TPU v7x, 32 devices: a whole 2x2x4 slice. The times are simulated.
32 devices in a mesh: groups: 2 (over y), seq: 4 (over z), chan: 2 (over x), sub: 2 (over core).
Axes of the slice: x: 2, y: 2, z: 4, core: 2. Of those that a mesh axis runs over, the one named last changes fastest.
Arguments:
- features: bfloat16 [1024, 96], P(('groups', 'seq'), 'chan'), parts along dimension 0, may hold values from -6 to 6
- proj: bfloat16 [96, 32], P('chan'), may hold values from -0.625 to 0.625
- kernel: float32 [2, 32, 9], P(None, 'chan'), may hold values from -2.4 to 2.4
- mix: bfloat16 [2, 32, 32], P(None, None, 'chan'), may hold values from -1 to 1
- readout: float32 [32], replicated, may hold values from -1 to 1
- dilations: int32 [2], replicated, may hold values from 1 to 8, as said below
- chrom_lengths: int32 [4], replicated, may hold values from 42 to 256, as said below
- pairs: int32 [32, 2], P(('groups', 'seq')), parts along dimension 0, may hold values from 0 to 3, as said below
- contact_cot: float32 [128, 1024], P('sub', ('groups', 'seq')), parts along dimension 1, may hold values from -6 to 6
- trans_cot: float32 [32, 128, 128], P(('groups', 'seq'), ('chan', 'sub')), parts along dimension 0, may hold values from -6 to 6
Outputs:
- contact: float32 [128, 1024], P('sub', ('groups', 'seq')), parts along dimension 1
- trans_maps: float32 [32, 128, 128], P(('groups', 'seq'), ('chan', 'sub')), parts along dimension 0
- grad_features: float32 [1024, 96], P(('groups', 'seq'), 'chan'), parts along dimension 0
- grad_proj: float32 [192, 32], P(('groups', 'chan')), parts along dimension 0
- grad_kernel: float32 [4, 32, 9], P('groups', 'chan'), parts along dimension 0
- grad_mix: float32 [4, 32, 32], P('groups', None, 'chan'), parts along dimension 0
There are 2 independent parts, one for each index of `groups`. A program takes and returns all parts, laid end to end along the dimension named above; an argument that names none is the same for every part. Nothing has to cross between parts.
Inputs may be any that keep to these rules, and one draw needn't show every extreme that they name: `dilations`: at least one layer has dilation 8. `chrom_lengths`: the lengths sum to 512; one is exactly 256 and one is exactly the least. `pairs`: the two blocks of a row differ; each block is the first block of exactly 4 rows.
All inputs are finite; a program needn't handle non-finite values.
Results may differ from a plain program's by a relative error of at most 0.006.
The roundings to bfloat16 on the way count: a program that leaves them out, or rounds other values in their place, can miss the bound.
Values may be sent and summed in bfloat16 or wider, within the bound.
A program may use at most 64 MiB of HBM per device.

v0:
```python
import jax
import jax.numpy as jnp
from jax import lax
from jax.sharding import PartitionSpec as P

DMAX = 8


HIGHEST_PRECISION = lax.Precision.HIGHEST


def shifted_2(value, axis, steps):
    count = lax.axis_size(axis)
    first, last = (max(0, -steps), min(count, count - steps))
    return lax.ppermute(value, axis, [(source, source + steps) for source in range(first, last)])


def with_halo(block, sides, width):
    for axis, dim in sides:
        count = lax.axis_size(axis)
        forward = [(i, i + 1) for i in range(count - 1)]
        backward = [(target, source) for source, target in forward]
        low = lax.ppermute(
            lax.slice_in_dim(block, block.shape[dim] - width, None, axis=dim), axis, forward
        )
        high = lax.ppermute(lax.slice_in_dim(block, 0, width, axis=dim), axis, backward)
        block = jnp.concatenate([low, block, high], axis=dim)
    return block


def chrom_of(positions, chrom_lengths, bin_limit):
    chrom_ends = jnp.cumsum(chrom_lengths)
    chrom_ids = jnp.sum((positions[..., None] >= chrom_ends).astype(jnp.int32), axis=-1)
    return jnp.where(positions < bin_limit, chrom_ids, -1)


def tap_offsets(dilation):
    result = []
    for across in (-1, 0, 1):
        for along in (-1, 0, 1):
            result.append((along * dilation, across * dilation))
    return result


def add_rows(accumulator, block_piece, row_start, column_start):
    anchor_rows = (row_start, column_start)
    current = lax.dynamic_slice(accumulator, anchor_rows, block_piece.shape)
    return lax.dynamic_update_slice(accumulator, current + block_piece, anchor_rows)


def per_device(
    features, proj, kernel, mix, readout, dilations, chrom_lengths, pairs, contact_cot, trans_cot
):
    bin_dev = features.shape[0]
    pair_width = proj.shape[1]
    chan_dev = kernel.shape[1]
    band_dev = contact_cot.shape[0]
    layers = kernel.shape[0]
    rows_trans = trans_cot.shape[1]
    seq_count = lax.axis_size("seq")
    band_total = band_dev * lax.axis_size("sub")
    total_bins = bin_dev * seq_count
    seq_pos = lax.axis_index("seq")
    chan_pos = lax.axis_index("chan")
    sub_pos = lax.axis_index("sub")
    first_chan = chan_pos * chan_dev
    first_diag = sub_pos * band_dev
    first_bin = seq_pos * bin_dev
    anchor = jnp.zeros((), jnp.int32)
    offsets = first_diag + jnp.arange(band_dev, dtype=jnp.int32)
    local_bins = first_bin + jnp.arange(bin_dev, dtype=jnp.int32)
    here_ids = chrom_of(local_bins, chrom_lengths, total_bins)
    there_ids = chrom_of(local_bins[None, :] + offsets[:, None], chrom_lengths, total_bins)
    band_mask = (here_ids[None, :] == there_ids).astype(jnp.float32)
    partial_profile = jnp.dot(features, proj, preferred_element_type=jnp.float32)
    profile = lax.psum(partial_profile, "chan")
    lookup_table = lax.all_gather(profile, "seq", axis=0, tiled=True)
    following = shifted_2(profile, "seq", -1)
    whole_rows = jnp.concatenate([profile, following], axis=0)
    own_cols = lax.dynamic_slice(profile, (anchor, first_chan), (bin_dev, chan_dev)).T
    reach_cols = lax.dynamic_slice(
        whole_rows, (anchor, first_chan), (bin_dev + band_total, chan_dev)
    ).T

    def build_pairs(own_part, reach_part):
        shifted = jax.vmap(
            lambda offset_value: lax.dynamic_slice_in_dim(reach_part, offset_value, bin_dev, 1),
            out_axes=1,
        )(offsets)
        return own_part[:, None, :] * shifted * band_mask[None]

    pair_field, build_back = jax.vjp(build_pairs, own_cols, reach_cols)
    saved_state = []
    for layer_id in range(layers):
        dilation = dilations[layer_id]
        tap_weights = kernel[layer_id]
        padded = with_halo(pair_field, (("seq", 2), ("sub", 1)), DMAX)
        mirrored = jnp.flip(padded[:, DMAX + 1 : 2 * DMAX + 1, :], axis=1)
        lower_rim = jnp.where(sub_pos == 0, mirrored, padded[:, :DMAX, :])
        padded = jnp.concatenate([lower_rim, padded[:, DMAX:, :]], axis=1)
        summed = jnp.zeros_like(pair_field)
        for tap_index, (along_off, across_off) in enumerate(tap_offsets(dilation)):
            corner = (anchor, DMAX + along_off, DMAX + across_off)
            window = lax.dynamic_slice(padded, corner, pair_field.shape)
            summed = summed + tap_weights[:, tap_index][:, None, None] * window
        hidden = jax.nn.relu(summed).astype(jnp.bfloat16)
        kept_inputs = lax.all_gather(hidden, "chan", axis=0, tiled=True)
        update = jnp.einsum(
            "ckn,ce->ekn", kept_inputs, mix[layer_id], preferred_element_type=jnp.float32
        )
        saved_state.append((padded, summed, kept_inputs, dilation))
        pair_field = (pair_field + update) * band_mask[None]
    weights_here = lax.dynamic_slice_in_dim(readout, first_chan, chan_dev, 0)
    contact_part = jnp.einsum("c,ckn->kn", weights_here, pair_field, precision=HIGHEST_PRECISION)
    contact = lax.psum(contact_part, "chan")
    row_start = (chan_pos * lax.axis_size("sub") + sub_pos) * rows_trans
    row_range = jnp.arange(rows_trans, dtype=jnp.int32)
    column_range = jnp.arange(bin_dev, dtype=jnp.int32)
    first_rows = jax.vmap(
        lambda block_id: lax.dynamic_slice_in_dim(
            lookup_table, block_id * bin_dev + row_start, rows_trans, 0
        )
    )(pairs[:, 0])
    second_rows = jax.vmap(
        lambda block_id: lax.dynamic_slice_in_dim(lookup_table, block_id * bin_dev, bin_dev, 0)
    )(pairs[:, 1])
    first_ids = chrom_of(
        pairs[:, 0:1] * bin_dev + row_start + row_range[None, :], chrom_lengths, total_bins
    )
    second_ids = chrom_of(
        pairs[:, 1:2] * bin_dev + column_range[None, :], chrom_lengths, total_bins
    )
    cross_mask = (first_ids[:, :, None] != second_ids[:, None, :]).astype(jnp.float32)
    weighted = first_rows * readout
    trans_maps = (
        jnp.einsum("prc,psc->prs", weighted, second_rows, precision=HIGHEST_PRECISION) * cross_mask
    )
    spent = trans_cot * cross_mask
    grad_first = (
        jnp.einsum("prs,psc->prc", spent, second_rows, precision=HIGHEST_PRECISION) * readout
    )
    grad_second = jnp.einsum("prs,prc->psc", spent, weighted, precision=HIGHEST_PRECISION)
    block_range = jnp.arange(seq_count, dtype=jnp.int32)
    hot_first = (pairs[:, 0:1] == block_range[None, :]).astype(jnp.float32)
    hot_second = (pairs[:, 1:2] == block_range[None, :]).astype(jnp.float32)
    first_part = jnp.einsum("pb,prc->brc", hot_first, grad_first, precision=HIGHEST_PRECISION)
    second_part = jnp.einsum("pb,psc->bsc", hot_second, grad_second, precision=HIGHEST_PRECISION)
    first_full = lax.dynamic_update_slice(
        jnp.zeros((seq_count, bin_dev, pair_width), jnp.float32),
        first_part,
        (anchor, row_start, anchor),
    )
    table_grad = (first_full + second_part).reshape(total_bins, pair_width)
    grad_field = weights_here[:, None, None] * contact_cot[None]
    kernel_grads = [None] * layers
    mix_grads_list = [None] * layers
    for layer_id in reversed(range(layers)):
        padded, summed, kept_inputs, dilation = saved_state[layer_id]
        grad_out = grad_field * band_mask[None]
        layer_mix = mix[layer_id]
        weight_rows = layer_mix.astype(jnp.float32)
        grad_hidden = lax.psum_scatter(
            jnp.einsum("ekn,ce->ckn", grad_out, weight_rows, precision=HIGHEST_PRECISION),
            "chan",
            scatter_dimension=0,
            tiled=True,
        ).astype(jnp.bfloat16)
        mix_grads_list[layer_id] = jnp.einsum(
            "ckn,ekn->ce", kept_inputs.astype(jnp.float32), grad_out, precision=HIGHEST_PRECISION
        )
        grad_sum = jnp.where(summed > 0, grad_hidden.astype(jnp.float32), 0.0)
        wide_grad = jnp.pad(grad_sum, ((0, 0), (2 * DMAX, 2 * DMAX), (2 * DMAX, 2 * DMAX)))
        grad_pad = jnp.zeros_like(padded)
        tap_grads = []
        for tap_index, (along_off, across_off) in enumerate(tap_offsets(dilation)):
            corner = (anchor, DMAX + along_off, DMAX + across_off)
            window = lax.dynamic_slice(padded, corner, grad_sum.shape)
            tap_grads.append(jnp.sum(window * grad_sum, axis=(1, 2)))
            moved = lax.dynamic_slice(
                wide_grad, (anchor, DMAX - along_off, DMAX - across_off), padded.shape
            )
            grad_pad = grad_pad + kernel[layer_id][:, tap_index][:, None, None] * moved
        kernel_grads[layer_id] = jnp.stack(tap_grads, axis=1)
        lower_rim = grad_pad[:, :DMAX, :]
        on_edge = sub_pos == 0
        folded = jnp.where(on_edge, jnp.flip(lower_rim, axis=1), 0.0)
        grad_pad = jnp.concatenate(
            [
                jnp.where(on_edge, 0.0, lower_rim),
                grad_pad[:, DMAX : DMAX + 1, :],
                grad_pad[:, DMAX + 1 : 2 * DMAX + 1, :] + folded,
                grad_pad[:, 2 * DMAX + 1 :, :],
            ],
            axis=1,
        )
        from_prev = shifted_2(grad_pad[:, :, -DMAX:], "seq", 1)
        from_next = shifted_2(grad_pad[:, :, :DMAX], "seq", -1)
        inner_part = grad_pad[:, :, DMAX:-DMAX]
        inner_width = inner_part.shape[2]
        inner_part = (
            inner_part
            + jnp.pad(from_prev, ((0, 0), (0, 0), (0, inner_width - DMAX)))
            + jnp.pad(from_next, ((0, 0), (0, 0), (inner_width - DMAX, 0)))
        )
        from_below = shifted_2(inner_part[:, -DMAX:, :], "sub", 1)
        from_above = shifted_2(inner_part[:, :DMAX, :], "sub", -1)
        middle = inner_part[:, DMAX:-DMAX, :]
        middle_rows = middle.shape[1]
        middle = (
            middle
            + jnp.pad(from_below, ((0, 0), (0, middle_rows - DMAX), (0, 0)))
            + jnp.pad(from_above, ((0, 0), (middle_rows - DMAX, 0), (0, 0)))
        )
        grad_field = grad_out + middle
    grad_own, grad_reach = build_back(grad_field)
    merged_back = grad_reach.T + jnp.pad(grad_own.T, ((0, band_total), (0, 0)))
    spread_back = lax.dynamic_update_slice(
        jnp.zeros((2 * bin_dev, pair_width), jnp.float32), merged_back, (anchor, first_chan)
    )
    band_part = spread_back[:bin_dev]
    next_piece = lax.dynamic_slice(
        spread_back, (anchor + bin_dev, first_chan), (band_total, chan_dev)
    )
    returned = shifted_2(next_piece, "seq", 1)
    band_part = add_rows(band_part, returned, anchor, first_chan)
    own_grad = lax.psum_scatter(table_grad, "seq", scatter_dimension=0, tiled=True)
    grad_profile = lax.psum(own_grad + band_part, ("chan", "sub"))
    grad_features = jnp.dot(grad_profile, proj.astype(jnp.float32).T, precision=HIGHEST_PRECISION)
    proj_part = jnp.dot(features.astype(jnp.float32).T, grad_profile, precision=HIGHEST_PRECISION)
    grad_proj = lax.psum(proj_part, "seq")
    kernel_stack = jnp.stack(kernel_grads, axis=0)
    mix_stack = jnp.stack(mix_grads_list, axis=0)
    grad_kernel, grad_mix = lax.psum((kernel_stack, mix_stack), ("seq", "sub"))
    return (contact, trans_maps, grad_features, grad_proj, grad_kernel, grad_mix)


def solution(mesh):
    in_specs = (
        P(("groups", "seq"), "chan"),
        P("chan", None),
        P(None, "chan", None),
        P(None, None, "chan"),
        P(),
        P(),
        P(),
        P(("groups", "seq"), None),
        P("sub", ("groups", "seq")),
        P(("groups", "seq"), ("chan", "sub"), None),
    )
    out_specs = (
        P("sub", ("groups", "seq")),
        P(("groups", "seq"), ("chan", "sub"), None),
        P(("groups", "seq"), "chan"),
        P(("groups", "chan"), None),
        P("groups", "chan", None),
        P("groups", None, "chan"),
    )
    return jax.shard_map(
        per_device, mesh=mesh, in_specs=in_specs, out_specs=out_specs, check_vma=False
    )
```

profile of v0, /device:TPU:0, one launch (start us, length us, event | category | flops | bytes accessed | tf_op | source)
XLA Modules:
  0.0 670.3 jit_solution(14410858774308351536)
XLA Ops:
  8.7 9.6 %psum.42 = f32[128,32]{0,1:T(8,128)S(1)} all-reduce(f32[128,32]{0,1:T(8,128)S(1)} %fusion.104), channel_id=1, replica_groups=mesh['groups'=2,'seq'=4,'chan'=2,'sub'=2] {'chan'}, use_global_device_ids=true, to_apply=%region_0.0 | all-reduce | flops 4096 | bytes 32768 | tf_op jit(solution)/shard_map/psum | solution.py:76
  21.6 2.4 convolution_bitcast_fusion.1
  24.0 14.5 %all_gather.11 = f32[512,32]{0,1:T(8,128)S(1)} all-gather(f32[128,32]{0,1:T(8,128)S(1)} %psum.42), channel_id=1, replica_groups=mesh['groups'=2,'seq'=4,'chan'=2,'sub'=2] {'seq'}, dimensions={0}, use_global_device_ids=true | all-gather | bytes 81920 | tf_op jit(solution)/shard_map/all_gather | solution.py:77
  39.3 7.5 %while.6 = (s32[]{:T(128)}, f32[512,32]{1,0:T(8,128)S(1)}, s32[4,2]{0,1:T(2,128)S(1)}, f32[4,128,32]{2,1,0:T(8,128)}, s32[]{:T(128)}) while((s32[]{:T(128)}, f32[512,32]{1,0:T(8,128)S(1)}, s32[4,2]{0,1:T(2,128)S(1)}, f32[4,128,32]{2,1,0:T(8,128)}, s32[]{:T(128)}) %tuple.132), condition=%wide.while_cond.2, body=%wide.while_body.2.sunk | while | flops 2 | bytes 82533 | solution.py:125
  46.9 84.0 %while.4 = (s32[]{:T(128)}, f32[16,256]{1,0:T(8,128)S(1)}, s32[64,2]{0,1:T(2,128)S(1)}, f32[64,16,128]{2,1,0:T(8,128)S(1)}, s32[]{:T(128)}) while((s32[]{:T(128)}, f32[16,256]{1,0:T(8,128)S(1)}, s32[64,2]{0,1:T(2,128)S(1)}, f32[64,16,128]{2,1,0:T(8,128)S(1)}, s32[]{:T(128)}) %tuple.129), condition=%wide.while_cond, body=%wide.while_body.sunk | while | flops 2 | bytes 16489 | solution.py:87
  131.9 3.4 collective-permute-start.1
  139.9 2.4 collective-permute-done.1
  142.3 4.1 collective-permute-done.2
  153.1 2.0 maximum_convert_fusion.1
  155.1 9.0 %all_gather.9 = bf16[32,64,128]{2,0,1:T(8,128)(2,1)S(1)} all-gather(bf16[16,64,128]{2,0,1:T(8,128)(2,1)S(1)} %get-tuple-element.181), channel_id=1, replica_groups=mesh['groups'=2,'seq'=4,'chan'=2,'sub'=2] {'chan'}, dimensions={0}, use_global_device_ids=true | all-gather | bytes 786432 | tf_op jit(solution)/shard_map/all_gather | solution.py:107
  165.5 2.8 collective-permute-start.5
  174.3 4.9 collective-permute-done.5
  179.2 4.3 collective-permute-done.6
  190.3 3.8 multiply_reduce_fusion
  194.1 3.2 fusion.8
  204.1 5.2 collective-permute-start.9
  223.4 5.1 while.5
  233.6 14.4 %all_gather.10 = bf16[32,64,128]{2,0,1:T(8,128)(2,1)S(1)} all-gather(bf16[16,64,128]{2,0,1:T(8,128)(2,1)S(1)} %maximum_convert_fusion), channel_id=1, replica_groups=mesh['groups'=2,'seq'=4,'chan'=2,'sub'=2] {'chan'}, dimensions={0}, use_global_device_ids=true | all-gather | bytes 786432 | tf_op jit(solution)/shard_map/all_gather | solution.py:107
  249.3 8.0 %psum.43 = f32[64,128]{1,0:T(8,128)} all-reduce(f32[64,128]{1,0:T(8,128)S(1)} %bitcast.183), channel_id=1, replica_groups=mesh['groups'=2,'seq'=4,'chan'=2,'sub'=2] {'chan'}, use_global_device_ids=true, to_apply=%region_4.5 | all-reduce | flops 8192 | bytes 65536 | tf_op jit(solution)/shard_map/psum | solution.py:115
  257.4 3.0 multiply_reduce_fusion.9
  260.5 3.2 fusion.25
  269.4 4.5 collective-permute-start.13
  286.5 316.2 %while.7 = (s32[]{:T(128)}, f32[16,256]{1,0:T(8,128)S(1)}, s32[64,2]{0,1:T(2,128)S(1)}, f32[64,16,128]{2,1,0:T(8,128)S(1)}, s32[]{:T(128)}, /*index=5*/s32[]{:T(128)}) while((s32[]{:T(128)}, f32[16,256]{1,0:T(8,128)S(1)}, s32[64,2]{0,1:T(2,128)S(1)}, f32[64,16,128]{2,1,0:T(8,128)S(1)}, s32[]{:T(128)}, /*index=5*/s32[]{:T(128)}) %tuple.138), condition=%wide.while_cond.3, body=%wide.while_body.3.sunk | while | flops 4109 | bytes 41095 | solution.py:87
  292.0 2.0 and_reduce_fusion.2
  297.0 2.0 and_reduce_fusion.2
  301.9 2.0 and_reduce_fusion.2
  306.9 2.0 and_reduce_fusion.2
  311.8 2.0 and_reduce_fusion.2
  316.7 2.0 and_reduce_fusion.2
  321.7 2.0 and_reduce_fusion.2
  326.6 2.0 and_reduce_fusion.2
  331.6 2.0 and_reduce_fusion.2
  336.5 2.0 and_reduce_fusion.2
  341.5 2.0 and_reduce_fusion.2
  371.1 2.0 and_reduce_fusion.2
  376.0 2.0 and_reduce_fusion.2
  381.0 2.0 and_reduce_fusion.2
  385.9 2.0 and_reduce_fusion.2
  390.9 2.0 and_reduce_fusion.2
  395.8 2.0 and_reduce_fusion.2
  400.8 2.0 and_reduce_fusion.2
  405.7 2.0 and_reduce_fusion.2
  410.6 2.0 and_reduce_fusion.2
  415.6 2.0 and_reduce_fusion.2
  602.8 4.3 collective-permute-start.17
  607.1 27.6 %all-reduce.14 = (f32[2,16,9]{1,2,0:T(8,128)S(1)}, f32[2,32,16]{1,2,0:T(8,128)}) all-reduce(f32[2,16,9]{1,2,0:T(8,128)S(1)} %pad_maximum_fusion.12, f32[2,32,16]{1,2,0:T(8,128)S(1)} %pad_maximum_fusion.13), channel_id=1, replica_groups=mesh['groups'=2,'seq'=4,'chan'=2,'sub'=2] {'seq','sub'}, use_global_device_ids=true, to_apply=%region_32.33 | all-reduce | flops 1312 | bytes 10496 | tf_op jit(solution)/shard_map/psum | solution.py:233
  636.1 10.1 %psum.44 = f32[128,32]{0,1:T(8,128)S(1)} all-reduce(f32[128,32]{0,1:T(8,128)S(1)} %add.698), channel_id=1, replica_groups=mesh['groups'=2,'seq'=4,'chan'=2,'sub'=2] {'chan','sub'}, use_global_device_ids=true, to_apply=%region_12.13 | all-reduce | flops 4096 | bytes 32768 | tf_op jit(solution)/shard_map/psum | solution.py:227
  647.2 16.6 %psum.45 = f32[48,32]{0,1:T(8,128)} all-reduce(f32[48,32]{0,1:T(8,128)S(1)} %convolution_bitcast_fusion.4), channel_id=1, replica_groups=mesh['groups'=2,'seq'=4,'chan'=2,'sub'=2] {'seq'}, use_global_device_ids=true, to_apply=%region_13.14 | all-reduce | flops 1536 | bytes 12288 | tf_op jit(solution)/shard_map/psum | solution.py:230
  (752 shorter events, 440.3 us)
Async XLA Ops:
  7.2 31.3 %copy-start.51 = (s32[4,2]{0,1:T(2,128)S(1)}, s32[4,2]{0,1:T(2,128)}, u32[]{:S(2)}) copy-start(s32[4,2]{0,1:T(2,128)} %param.17) | copy-start | bytes 100
  7.2 32.0 %copy-start.17 = (f32[2,16,9]{1,0,2:T(2,128)S(1)}, f32[2,16,9]{1,0,2:T(2,128)}, u32[]{:S(2)}) copy-start(f32[2,16,9]{1,0,2:T(2,128)} %param.12) | copy-start | bytes 3460
  7.2 183.1 %reduce-scatter.6.cloned.1.call-start = ((), (), s32[]{:S(2)}) async-start(), calls=%async_computation.4 | async-start | bytes 1572864 | tf_op jit(solution)/shard_map/reduce_scatter | solution.py:162
  18.3 28.6 %collective-permute-start = (f32[128,32]{0,1:T(8,128)S(1)}, f32[128,32]{0,1:T(8,128)S(1)}, u32[]{:S(2)}, u32[]{:S(2)}) collective-permute-start(f32[128,32]{0,1:T(8,128)S(1)} %psum.42), channel_id=1, source_target_pairs={{4,0},{8,4},{12,8},{5,1},{9,5},{13,9},{6,2},{10,6},{14,10},{7,3},{... | collective-permute-start | bytes 49160 | tf_op jit(solution)/shard_map/ppermute | solution.py:15
  24.0 233.4 %reduce-scatter.8.cloned.1.call-start = ((), (), s32[]{:S(2)}) async-start(), calls=%async_computation.5 | async-start | bytes 1572864 | tf_op jit(solution)/shard_map/reduce_scatter | solution.py:162
  39.1 92.8 %copy-start.27 = (s32[4]{0:T(128)}, s32[4]{0:T(128)S(1)}, u32[]{:S(2)}) copy-start(s32[4]{0:T(128)S(1)} %get-tuple-element.215) | copy-start | bytes 52
  130.9 22.2 %copy-start.1 = (f32[64,16,128]{2,1,0:T(8,128)}, f32[64,16,128]{2,1,0:T(8,128)S(1)}, u32[]{:S(2)}) copy-start(f32[64,16,128]{2,1,0:T(8,128)S(1)} %get-tuple-element.13) | copy-start | bytes 1572868
  130.9 5.8 copy-start.40
  131.9 10.4 %collective-permute-start.1 = (f32[16,64,8]{2,0,1:T(8,128)}, f32[16,64,8]{2,0,1:T(8,128)S(1)}, u32[]{:S(2)}, u32[]{:S(2)}) collective-permute-start(f32[16,64,8]{2,0,1:T(8,128)} %get-tuple-element.207), channel_id=1, source_target_pairs={{0,4},{4,8},{8,12},{1,5},{5,9},{9,13},{2,6},{6,10},{10,14},{3,7},{... | collective-permute-start | bytes 98312 | tf_op jit(solution)/shard_map/ppermute | solution.py:23
  135.4 11.1 %collective-permute-start.2 = (f32[16,64,8]{2,0,1:T(8,128)S(1)}, f32[16,64,8]{2,0,1:T(8,128)S(1)}, u32[]{:S(2)}, u32[]{:S(2)}) collective-permute-start(f32[16,64,8]{2,0,1:T(8,128)S(1)} %get-tuple-element.208), channel_id=1, source_target_pairs={{4,0},{8,4},{12,8},{5,1},{9,5},{13,9},{6,2},{10,6},{14,10},{7,3},{... | collective-permute-start | bytes 98312 | tf_op jit(solution)/shard_map/ppermute | solution.py:26
  146.7 2.9 collective-permute-start.3
  148.3 3.2 collective-permute-start.4
  153.1 11.0 %copy-start.16 = (bf16[2,32,16]{1,2,0:T(8,128)(2,1)S(1)}, bf16[2,32,16]{1,2,0:T(8,128)(2,1)}, u32[]{:S(2)}) copy-start(bf16[2,32,16]{1,2,0:T(8,128)(2,1)} %param.13) | copy-start | bytes 6148
  165.5 13.8 %collective-permute-start.5 = (f32[16,64,8]{2,0,1:T(8,128)}, f32[16,64,8]{2,0,1:T(8,128)S(1)}, u32[]{:S(2)}, u32[]{:S(2)}) collective-permute-start(f32[16,64,8]{2,0,1:T(8,128)} %get-tuple-element.205), channel_id=1, source_target_pairs={{0,4},{4,8},{8,12},{1,5},{5,9},{9,13},{2,6},{6,10},{10,14},{3,7},{... | collective-permute-start | bytes 98312 | tf_op jit(solution)/shard_map/ppermute | solution.py:23
  168.3 15.2 %collective-permute-start.6 = (f32[16,64,8]{2,0,1:T(8,128)}, f32[16,64,8]{2,0,1:T(8,128)S(1)}, u32[]{:S(2)}, u32[]{:S(2)}) collective-permute-start(f32[16,64,8]{2,0,1:T(8,128)} %get-tuple-element.206), channel_id=1, source_target_pairs={{4,0},{8,4},{12,8},{5,1},{9,5},{13,9},{6,2},{10,6},{14,10},{7,3},{... | collective-permute-start | bytes 98312 | tf_op jit(solution)/shard_map/ppermute | solution.py:26
  179.2 7.5 %copy-start.9 = (f32[16,64,8]{2,0,1:T(8,128)}, f32[16,64,8]{2,0,1:T(8,128)S(1)}, u32[]{:S(2)}) copy-start(f32[16,64,8]{2,0,1:T(8,128)S(1)} %collective-permute-done.5) | copy-start | bytes 98308
  183.7 2.9 collective-permute-start.7
  185.3 3.2 collective-permute-start.8
  198.8 10.4 %copy-start.28 = (s32[4]{0:T(128)S(1)}, s32[4]{0:T(128)}, u32[]{:S(2)}) copy-start(s32[4]{0:T(128)} %copy-done.27) | copy-start | bytes 52
  202.8 10.0 %collective-permute-start.10 = (f32[16,80,8]{1,2,0:T(8,128)}, f32[16,80,8]{1,2,0:T(8,128)}, u32[]{:S(2)}, u32[]{:S(2)}) collective-permute-start(f32[16,80,8]{1,2,0:T(8,128)} %copy.72), channel_id=1, source_target_pairs={{4,0},{8,4},{12,8},{5,1},{9,5},{13,9},{6,2},{10,6},{14,10},{7,3},{... | collective-permute-start | bytes 122888 | tf_op jit(solution)/shard_map/ppermute | solution.py:15
  204.1 6.8 %collective-permute-start.9 = (f32[16,80,8]{1,2,0:T(8,128)}, f32[16,80,8]{1,2,0:T(8,128)}, u32[]{:S(2)}, u32[]{:S(2)}) collective-permute-start(f32[16,80,8]{1,2,0:T(8,128)} %copy.70), channel_id=1, source_target_pairs={{0,4},{4,8},{8,12},{1,5},{5,9},{9,13},{2,6},{6,10},{10,14},{3,7},{... | collective-permute-start | bytes 122888 | tf_op jit(solution)/shard_map/ppermute | solution.py:15
  214.8 6.2 copy-start.14
  216.5 2.7 collective-permute-start.11
  217.8 3.1 collective-permute-start.12
  222.6 6.2 copy-start.30
  222.6 6.4 copy-start.29
  222.7 10.9 %copy-start.12 = (bf16[16,64,128]{2,0,1:T(8,128)(2,1)S(1)}, bf16[16,64,128]{2,0,1:T(8,128)(2,1)}, u32[]{:S(2)}) copy-start(bf16[16,64,128]{2,0,1:T(8,128)(2,1)} %get-tuple-element.180) | copy-start | bytes 786436
  222.7 412.7 %reduce-scatter.4.cloned.1.call-start = ((), (), s32[]{:S(2)}) async-start(), calls=%async_computation.3 | async-start | bytes 81920 | tf_op jit(solution)/shard_map/reduce_scatter | solution.py:226
  248.0 9.3 %copy-start.31 = (f32[16]{0:T(128)S(1)}, f32[16]{0:T(128)}, u32[]{:S(2)}) copy-start(f32[16]{0:T(128)} %get-tuple-element.116) | copy-start | bytes 196
  248.0 9.3 %copy-start.32 = (f32[16]{0:T(128)S(1)}, f32[16]{0:T(128)}, u32[]{:S(2)}) copy-start(f32[16]{0:T(128)} %get-tuple-element.117) | copy-start | bytes 196
  248.0 9.3 %copy-start.33 = (f32[16]{0:T(128)S(1)}, f32[16]{0:T(128)}, u32[]{:S(2)}) copy-start(f32[16]{0:T(128)} %get-tuple-element.118) | copy-start | bytes 196
  248.0 9.3 %copy-start.34 = (f32[16]{0:T(128)S(1)}, f32[16]{0:T(128)}, u32[]{:S(2)}) copy-start(f32[16]{0:T(128)} %get-tuple-element.119) | copy-start | bytes 196
  248.0 9.3 %copy-start.35 = (f32[16]{0:T(128)S(1)}, f32[16]{0:T(128)}, u32[]{:S(2)}) copy-start(f32[16]{0:T(128)} %get-tuple-element.120) | copy-start | bytes 196
  248.0 9.3 %copy-start.36 = (f32[16]{0:T(128)S(1)}, f32[16]{0:T(128)}, u32[]{:S(2)}) copy-start(f32[16]{0:T(128)} %get-tuple-element.121) | copy-start | bytes 196
  248.1 9.3 %copy-start.37 = (f32[16]{0:T(128)S(1)}, f32[16]{0:T(128)}, u32[]{:S(2)}) copy-start(f32[16]{0:T(128)} %get-tuple-element.122) | copy-start | bytes 196
  248.1 9.3 %copy-start.38 = (f32[16]{0:T(128)S(1)}, f32[16]{0:T(128)}, u32[]{:S(2)}) copy-start(f32[16]{0:T(128)} %get-tuple-element.123) | copy-start | bytes 196
  248.1 9.3 %copy-start.39 = (f32[16]{0:T(128)S(1)}, f32[16]{0:T(128)}, u32[]{:S(2)}) copy-start(f32[16]{0:T(128)} %get-tuple-element.125) | copy-start | bytes 196
  248.1 9.3 %copy-start.2 = (f32[64,16,128]{2,1,0:T(8,128)S(1)}, f32[64,16,128]{2,1,0:T(8,128)}, u32[]{:S(2)}) copy-start(f32[64,16,128]{2,1,0:T(8,128)} %copy-done.1) | copy-start | bytes 1572868
  248.3 9.1 %copy-start.8 = (f32[16,64,128]{2,0,1:T(8,128)S(1)}, f32[16,64,128]{2,0,1:T(8,128)}, u32[]{:S(2)}) copy-start(f32[16,64,128]{2,0,1:T(8,128)} %get-tuple-element.182) | copy-start | bytes 1572868
  265.3 8.6 %copy-start.4 = (f32[16,80,128]{2,0,1:T(8,128)S(1)}, f32[16,80,128]{2,0,1:T(8,128)}, u32[]{:S(2)}) copy-start(f32[16,80,128]{2,0,1:T(8,128)} %copy-done.3) | copy-start | bytes 1966084
  265.3 8.7 %copy-start.7 = (bf16[32,64,128]{2,0,1:T(8,128)(2,1)S(1)}, bf16[32,64,128]{2,0,1:T(8,128)(2,1)}, u32[]{:S(2)}) copy-start(bf16[32,64,128]{2,0,1:T(8,128)(2,1)} %copy-done.6) | copy-start | bytes 1572868
  268.1 8.9 %collective-permute-start.14 = (f32[16,80,8]{1,2,0:T(8,128)S(1)}, f32[16,80,8]{1,2,0:T(8,128)S(1)}, u32[]{:S(2)}, u32[]{:S(2)}) collective-permute-start(f32[16,80,8]{1,2,0:T(8,128)S(1)} %copy.76), channel_id=1, source_target_pairs={{4,0},{8,4},{12,8},{5,1},{9,5},{13,9},{6,2},{10,6},{14,10},{7,3},{... | collective-permute-start | bytes 122888 | tf_op jit(solution)/shard_map/ppermute | solution.py:15
  269.4 6.4 collective-permute-start.13
  278.1 5.3 copy-start.46
  280.8 2.8 collective-permute-start.15
  282.1 3.1 collective-permute-start.16
  283.5 362.8 %copy-start.18 = (bf16[48,32]{0,1:T(8,128)(2,1)S(1)}, bf16[48,32]{0,1:T(8,128)(2,1)}, u32[]{:S(2)}) copy-start(bf16[48,32]{0,1:T(8,128)(2,1)} %param.11) | copy-start | bytes 9220
  602.8 32.5 %collective-permute-start.17 = (f32[128,16]{0,1:T(8,128)S(1)}, f32[128,16]{0,1:T(8,128)S(1)}, u32[]{:S(2)}, u32[]{:S(2)}) collective-permute-start(f32[128,16]{0,1:T(8,128)S(1)} %constant_dynamic-slice_fusion.6), channel_id=1, source_target_pairs={{0,4},{4,8},{8,12},{1,5},{5,9},{9,13},{2,6},{6,10},{10,14},{3,7},{... | collective-permute-start | bytes 24584 | tf_op jit(solution)/shard_map/ppermute | solution.py:15
  (25 other events, 98.8 us)
Sparse Core Ops, SparseCore 0:
  24.1 21.6 reduce-scatter.5
  222.8 22.9 reduce-scatter.7
  248.1 18.3 reduce-scatter.3
where the time goes:
time: 675 us; the launch traced here: 670 us
  other arithmetic  243 us (36%)
  local copies, waits for them, and re-layouts  220 us (33%)
  blocking collectives  110 us (16%)
  starting transfers between devices  37.1 us (5%)
  waiting for transfers between devices  25.8 us (4%)
  between operations  23.9 us (4%)
  matrix products  10.1 us (1%)
    scatter-add x128, other arithmetic  215 us
    scatter-add x192, local copies, waits for them, and re-layouts  100 us
    gather x216, local copies, waits for them, and re-layouts  96.3 us
    psum x1, blocking collectives, per_device(): grad_kernel, grad_mix = lax.psum((kernel_stack, mix_stack), ('seq', 'sub'))  27.6 us
    all_gather x2, blocking collectives, per_device(): kept_inputs = lax.all_gather(hidden, 'chan', axis=0, tiled=True)  23.4 us
    ppermute x10, starting transfers between devices, shifted_2(): lax.ppermute(value, axis, [(source, source + steps) for source in range(f...  23 us
    psum x1, blocking collectives, per_device(): grad_proj = lax.psum(proj_part, 'seq')  16.6 us
    all_gather x1, blocking collectives, per_device(): lookup_table = lax.all_gather(profile, 'seq', axis=0, tiled=True)  14.5 us
  transfers between devices with their start and end apart: 21, of which 10 were waited for; matrix products, arithmetic and copies ran while one was open for 67% of the time, Pallas kernels for 0%

commit v1 on v0

v1 whole, which is shorter than its diff:
```python
import jax
import jax.numpy as jnp
from jax import lax
from jax.experimental import pallas as pl
from jax.experimental.pallas import tpu as pltpu
from jax.sharding import PartitionSpec as P

HALO = 8
LANES = 128
GUARD = 32
LOW = 16
BATCH = 8
EXACT = lax.Precision.HIGHEST
NT = (((1,), (1,)), ((), ()))
NN = (((1,), (0,)), ((), ()))


def mm(a, b, dims=NN, precision=None):
    return lax.dot_general(a, b, dims, precision=precision, preferred_element_type=jnp.float32)


def split(value):
    high = value.astype(jnp.bfloat16)
    return high, (value - high.astype(jnp.float32)).astype(jnp.bfloat16)


def band_kernel(
    dil, chroms, pairs, feats, proj, proj_t, mix, mix_t, taps_in, ro_col, ro_row, cot, tcot,
    contact, maps, grads, gproj_t, gtaps, gmix,
    taps, spread, env, prof, prof_t, x0, x1, h, go, gs, gf, go1, gs1, gpad, acc, spent,
):
    chans = proj.shape[1]
    layers = mix.shape[0]
    bin_dev = LANES
    seq_count, chan_count = lax.axis_size("seq"), lax.axis_size("chan")
    seq_pos, chan_pos, sub_pos = lax.axis_index("seq"), lax.axis_index("chan"), lax.axis_index("sub")
    total = seq_count * bin_dev
    own_bins = bin_dev // chan_count
    rows = h.shape[1]
    own_rows = rows - 3 * HALO
    wide = BATCH * chans
    first = seq_pos * bin_dev + chan_pos * own_bins - GUARD
    k_base = sub_pos * (own_rows - 3 * HALO)
    own_start = sub_pos * 3 * HALO
    is_low = (sub_pos == 0).astype(jnp.float32)

    ends, run = [], jnp.int32(0)
    for j in range(chroms.shape[0]):
        run = run + chroms[j]
        ends.append(run)

    def end_of(pos):
        best = jnp.full(pos.shape, 1 << 20, jnp.int32)
        for e in ends:
            best = jnp.minimum(best, jnp.where(pos < e, e, 1 << 20))
        return best

    pos = first + lax.broadcasted_iota(jnp.int32, (1, LANES), 1)
    left = jnp.where((pos >= 0) & (pos < total), end_of(pos) - pos, 0)
    lane = lax.broadcasted_iota(jnp.int32, (1, LANES), 1)
    own_lane = ((lane >= GUARD) & (lane < GUARD + own_bins)).astype(jnp.float32)

    def mask(r):
        return (k_base + r < left).astype(jnp.float32)

    r_i = lax.broadcasted_iota(jnp.int32, (wide, chans), 0)
    c_i = lax.broadcasted_iota(jnp.int32, (wide, chans), 1)
    fan = (lax.rem(r_i, chans) == c_i).astype(jnp.bfloat16)
    r_w = lax.broadcasted_iota(jnp.int32, (wide, wide), 0) // chans
    c_w = lax.broadcasted_iota(jnp.int32, (wide, wide), 1) // chans
    diag = r_w == c_w
    for l in range(layers):
        for side, source in enumerate((mix_t, mix)):
            tall = mm(fan, source[l]).astype(jnp.bfloat16)
            full = mm(tall, fan, NT)
            spread[2 * l + side] = jnp.where(diag, full, 0.0).astype(jnp.bfloat16)
        for t in range(9):
            taps[l, t] = jnp.broadcast_to(taps_in[l][:, t : t + 1], (chans, LANES))

    prof[...] = mm(feats[pl.ds(LANES, total), :], proj[...])
    for b in range(seq_count):
        prof_t[b] = mm(proj_t[...], feats[(b + 1) * LANES : (b + 2) * LANES, :], NT)
    start = pl.multiple_of(first + LANES, 16)
    env[...] = mm(proj_t[...], feats[pl.ds(start, 2 * LANES), :], NT)
    ro = jnp.broadcast_to(ro_col[...], (chans, LANES))

    for buf in (x0, x1, gs, gs1):
        for r in (*range(LOW), *range(LOW + rows, 2 * LOW + rows)):
            buf[r] = jnp.zeros((chans, LANES), jnp.float32)

    def clear(i, _):
        gs[LOW + i] = jnp.zeros((chans, LANES), jnp.float32)
        gs1[LOW + i] = jnp.zeros((chans, LANES), jnp.float32)
        go1[i] = jnp.zeros((chans, LANES), jnp.float32)
        return 0

    lax.fori_loop(0, rows, clear, 0, unroll=4)

    def build(i, _):
        k = k_base + i
        moved = pltpu.roll(env[...], lax.rem(2 * LANES - k, 2 * LANES), 1)[:, :LANES]
        x0[LOW + i] = env[:, :LANES] * moved * mask(i)
        return 0

    lax.fori_loop(0, rows, build, 0, unroll=4)

    def conv(x, l, d, r, sign):
        lines = [x[LOW + r + sign * b * d] for b in (-1, 0, 1)]
        sums = []
        for a in range(3):
            t = [taps[l, 3 * a + b] * lines[b] for b in range(3)]
            sums.append(t[0] + t[1] + t[2])
        fwd, back = (d, LANES - d) if sign > 0 else (LANES - d, d)
        return sums[1] + pltpu.roll(sums[0], fwd, 1) + pltpu.roll(sums[2], back, 1)

    xs = [x0, x1]
    for l in range(layers):
        d = dil[l]
        x = xs[l]
        for m in range(1, HALO + 1):
            x[LOW - m] = x[LOW + m]
        base = sub_pos * HALO * (l + 1)

        def layer(i, _, l=l, d=d, x=x, base=base):
            r0 = base + i * BATCH
            for j in range(BATCH):
                summed = conv(x, l, d, r0 + j, 1)
                h[l, r0 + j] = jnp.maximum(summed, 0.0).astype(jnp.bfloat16)
            upd = mm(spread[2 * l], h[l, pl.ds(r0, BATCH)].reshape(wide, LANES))
            upd = upd.reshape(BATCH, chans, LANES)
            for j in range(BATCH):
                new = (x[LOW + r0 + j] + upd[j]) * mask(r0 + j)
                if l + 1 < layers:
                    xs[l + 1][LOW + r0 + j] = new
                else:
                    contact[pl.ds(i * BATCH + j, 1), :] = jnp.sum(new * ro, axis=0, keepdims=True)
            return 0

        lax.fori_loop(0, (rows - HALO * (l + 1)) // BATCH, layer, 0)

    def pull(l, r0, source, target):
        g = source[pl.ds(r0, BATCH)].reshape(wide, LANES)
        high, low = split(g)
        gh = mm(spread[2 * l + 1], high) + mm(spread[2 * l + 1], low)
        gh = gh.astype(jnp.bfloat16).astype(jnp.float32).reshape(BATCH, chans, LANES)
        for j in range(BATCH):
            on = h[l, r0 + j].astype(jnp.float32) > 0
            target[LOW + r0 + j] = jnp.where(on, gh[j], 0.0)

    def weight_grads(l, x, d, g_out, g_sum):
        acc[...] = jnp.zeros_like(acc)

        def body(i, sums):
            r0 = own_start + i * BATCH
            g = (g_out[pl.ds(r0, BATCH)] * own_lane).astype(jnp.bfloat16).reshape(wide, LANES)
            acc[...] += mm(h[l, pl.ds(r0, BATCH)].reshape(wide, LANES), g, NT)
            for j in range(BATCH):
                r = r0 + j
                g0 = g_sum[LOW + r] * own_lane
                moved = (pltpu.roll(g0, LANES - d, 1), g0, pltpu.roll(g0, d, 1))
                lines = [x[LOW + r + b * d] for b in (-1, 0, 1)]
                sums = tuple(sums[t] + moved[t // 3] * lines[t % 3] for t in range(9))
            return sums

        zero = jnp.zeros((chans, LANES), jnp.float32)
        sums = lax.fori_loop(0, own_rows // BATCH, body, (zero,) * 9)
        for t in range(9):
            gtaps[l, :, t : t + 1] = jnp.sum(sums[t], axis=1, keepdims=True)
        tall = jnp.sum(jnp.where(diag, acc[...], 0.0).reshape(BATCH, chans, wide), axis=0)
        gmix[l] = mm(tall, fan.astype(jnp.float32), precision=EXACT)

    def last_out(i, _):
        r0 = sub_pos * 2 * HALO + i * BATCH
        for j in range(BATCH):
            line = cot[pl.ds(i * BATCH + j, 1), :] * mask(r0 + j)
            go[r0 + j] = ro * line
        pull(1, r0, go, gs)
        return 0

    lax.fori_loop(0, (rows - 2 * HALO) // BATCH, last_out, 0)
    weight_grads(1, x1, dil[1], go, gs)

    def fold(l, d, g, target):
        for m in range(1, HALO + 1):
            target[m] = target[m] + is_low * conv(g, l, d, -m, -1)

    def back_field(i, _):
        r0 = own_start + i * BATCH
        for j in range(BATCH):
            gf[r0 + j] = go[r0 + j] + conv(gs, 1, dil[1], r0 + j, -1)
        return 0

    lax.fori_loop(0, own_rows // BATCH, back_field, 0)
    fold(1, dil[1], gs, gf)

    def first_out(i, _):
        r0 = own_start + i * BATCH
        for j in range(BATCH):
            go1[r0 + j] = gf[r0 + j] * (mask(r0 + j) * own_lane)
        pull(0, r0, go1, gs1)
        return 0

    lax.fori_loop(0, own_rows // BATCH, first_out, 0)
    weight_grads(0, x0, dil[0], go1, gs1)

    def back_first(i, _):
        r0 = sub_pos * 2 * HALO + i * BATCH
        for j in range(BATCH):
            gf[r0 + j] = go1[r0 + j] + conv(gs1, 0, dil[0], r0 + j, -1)
        return 0

    lax.fori_loop(0, (rows - 2 * HALO) // BATCH, back_first, 0)
    fold(0, dil[0], gs1, gf)

    def to_profile(i, carry):
        near, far = carry
        r = sub_pos * 2 * HALO + i
        k = k_base + r
        g = gf[r] * mask(r)
        moved = pltpu.roll(env[...], lax.rem(2 * LANES - k, 2 * LANES), 1)[:, :LANES]
        near = near + g * moved
        part = jnp.concatenate([g * env[:, :LANES], jnp.zeros((chans, LANES), jnp.float32)], axis=1)
        far = far + pltpu.roll(part, k, 1)
        return near, far

    near, far = lax.fori_loop(
        0, rows - 2 * HALO, to_profile,
        (jnp.zeros((chans, LANES), jnp.float32), jnp.zeros((chans, 2 * LANES), jnp.float32)),
    )
    near = far[:, :LANES] + near
    zero = jnp.zeros((chans, LANES), jnp.float32)
    whole = jnp.concatenate([near, far[:, LANES:], zero], axis=1)
    place = first + LANES
    tile = place // LANES
    whole = pltpu.roll(whole, lax.rem(place, LANES), 1)
    for b in range(gpad.shape[0]):
        gpad[b] = zero
    for b in range(3):
        gpad[tile + b] = whole[:, b * LANES : (b + 1) * LANES]

    rows_trans = tcot.shape[1]
    row_start = pl.multiple_of((chan_pos * 2 + sub_pos) * rows_trans, 8)
    for n in range(tcot.shape[0]):
        p, q = pairs[n, 0], pairs[n, 1]
        first_rows = prof[pl.ds(pl.multiple_of(p * LANES + row_start, 8), rows_trans), :] * ro_row[...]
        second = prof[pl.ds(pl.multiple_of(q * LANES, 8), LANES), :]
        row_pos = p * LANES + row_start + lax.broadcasted_iota(jnp.int32, (rows_trans, LANES), 0)
        col_pos = q * LANES + lax.broadcasted_iota(jnp.int32, (rows_trans, LANES), 1)
        cross = (end_of(row_pos) != end_of(col_pos)).astype(jnp.float32)
        maps[n] = mm(first_rows, second, NT, EXACT) * cross
        spent[...] = jnp.zeros_like(spent)
        spent[pl.ds(row_start, rows_trans), :] = tcot[n] * cross
        to_first = mm(prof_t[q], spent[...], NT, EXACT) * ro
        to_second = mm(prof_t[p] * ro, spent[...], NN, EXACT)
        gpad[1 + p] = gpad[1 + p] + to_first
        gpad[1 + q] = gpad[1 + q] + to_second

    total_proj = jnp.zeros(gproj_t.shape, jnp.float32)
    for b in range(seq_count):
        g = gpad[1 + b]
        grads[b] = g
        high, low = split(g)
        block = feats[(b + 1) * LANES : (b + 2) * LANES, :]
        total_proj = total_proj + mm(high, block) + mm(low, block)
    gproj_t[...] = total_proj


def per_device(
    features, proj, kernel, mix, readout, dilations, chrom_lengths, pairs, contact_cot, trans_cot
):
    bin_dev = features.shape[0]
    chans = proj.shape[1]
    band_dev = contact_cot.shape[0]
    layers = kernel.shape[0]
    seq_count, chan_count = lax.axis_size("seq"), lax.axis_size("chan")
    seq_pos, chan_pos, sub_pos = lax.axis_index("seq"), lax.axis_index("chan"), lax.axis_index("sub")
    own_bins = bin_dev // chan_count
    total = bin_dev * seq_count
    rows = band_dev + 3 * HALO

    feats = lax.all_gather(features, ("seq", "chan"), axis=0)
    feats = feats.reshape(seq_count, chan_count, bin_dev, -1).transpose(0, 2, 1, 3)
    feats = jnp.pad(feats.reshape(total, -1), ((bin_dev, 2 * bin_dev), (0, 0)))
    proj_all = lax.all_gather(proj, "chan", axis=0, tiled=True)
    mix_all = lax.all_gather(mix, "chan", axis=2, tiled=True)
    taps = lax.all_gather(kernel, "chan", axis=1, tiled=True)
    edge = jnp.where(sub_pos == 0, contact_cot[-HALO:], contact_cot[:HALO])
    edge = lax.ppermute(edge, "sub", [(0, 1), (1, 0)])
    zeros = jnp.zeros_like(edge)
    cot = jnp.where(
        sub_pos == 0,
        jnp.concatenate([contact_cot, edge], axis=0),
        jnp.concatenate([edge, contact_cot], axis=0),
    )
    side = jnp.where(chan_pos == 0, cot[:, -HALO:], cot[:, :HALO])
    moves = []
    for s in range(seq_count - 1):
        moves.append((s * chan_count, (s + 1) * chan_count))
        moves.append(((s + 2) * chan_count - 1, (s + 1) * chan_count - 1))
    side = lax.ppermute(side, ("seq", "chan"), moves)
    blank = jnp.zeros((cot.shape[0], GUARD - HALO), jnp.float32)
    cot = jnp.concatenate([blank, side, cot, side, blank], axis=1)
    cot = lax.dynamic_slice_in_dim(cot, chan_pos * own_bins, LANES, 1)

    f32 = jnp.float32
    smem = pl.BlockSpec(memory_space=pltpu.SMEM)
    vmem = pl.BlockSpec(memory_space=pltpu.VMEM)
    field = pltpu.VMEM((2 * LOW + rows, chans, LANES), f32)
    plain = pltpu.VMEM((rows, chans, LANES), f32)
    wide = BATCH * chans
    width = proj_all.shape[0]
    contact, maps, grads, gproj_t, gtaps, gmix = pl.pallas_call(
        band_kernel,
        out_shape=(
            jax.ShapeDtypeStruct((band_dev + HALO, LANES), f32),
            jax.ShapeDtypeStruct(trans_cot.shape, f32),
            jax.ShapeDtypeStruct((seq_count, chans, LANES), f32),
            jax.ShapeDtypeStruct((chans, width), f32),
            jax.ShapeDtypeStruct((layers, chans, 9), f32),
            jax.ShapeDtypeStruct((layers, chans, chans), f32),
        ),
        in_specs=[smem] * 3 + [vmem] * 10,
        out_specs=(vmem,) * 6,
        scratch_shapes=[
            pltpu.VMEM((layers, 9, chans, LANES), f32),
            pltpu.VMEM((2 * layers, wide, wide), jnp.bfloat16),
            pltpu.VMEM((chans, 2 * LANES), f32),
            pltpu.VMEM((total, chans), f32),
            pltpu.VMEM((seq_count, chans, LANES), f32),
            field,
            field,
            pltpu.VMEM((layers, rows, chans, LANES), jnp.bfloat16),
            plain,
            field,
            plain,
            plain,
            field,
            pltpu.VMEM((seq_count + 3, chans, LANES), f32),
            pltpu.VMEM((wide, wide), f32),
            pltpu.VMEM((LANES, LANES), f32),
        ],
        compiler_params=pltpu.CompilerParams(vmem_limit_bytes=48 * 1024 * 1024),
    )(
        dilations, chrom_lengths, pairs, feats, proj_all, proj_all.T, mix_all,
        mix_all.transpose(0, 2, 1), taps, readout[:, None], readout[None, :], cot, trans_cot,
    )
    everyone = ("seq", "chan", "sub")
    grads, gproj_t, gtaps, gmix = lax.psum((grads, gproj_t, gtaps, gmix), everyone)
    own = lax.dynamic_index_in_dim(grads, seq_pos, 0, keepdims=False)
    grad_features = lax.dot_general(
        own, proj.astype(f32), (((0,), (1,)), ((), ())), precision=EXACT
    )
    chan_dev, width_dev = kernel.shape[1], proj.shape[0]
    grad_proj = lax.dynamic_slice_in_dim(gproj_t, chan_pos * width_dev, width_dev, 1).T
    grad_kernel = lax.dynamic_slice_in_dim(gtaps, chan_pos * chan_dev, chan_dev, 1)
    grad_mix = lax.dynamic_slice_in_dim(gmix, chan_pos * chan_dev, chan_dev, 2)
    contact = lax.dynamic_slice(
        contact, (sub_pos * HALO, jnp.int32(GUARD)), (band_dev, own_bins)
    )
    contact = lax.all_gather(contact, "chan", axis=1, tiled=True)
    return (contact, maps, grad_features, grad_proj, grad_kernel, grad_mix)


def solution(mesh):
    in_specs = (
        P(("groups", "seq"), "chan"),
        P("chan", None),
        P(None, "chan", None),
        P(None, None, "chan"),
        P(),
        P(),
        P(),
        P(("groups", "seq"), None),
        P("sub", ("groups", "seq")),
        P(("groups", "seq"), ("chan", "sub"), None),
    )
    out_specs = (
        P("sub", ("groups", "seq")),
        P(("groups", "seq"), ("chan", "sub"), None),
        P(("groups", "seq"), "chan"),
        P(("groups", "chan"), None),
        P("groups", "chan", None),
        P("groups", None, "chan"),
    )
    return jax.shard_map(
        per_device, mesh=mesh, in_specs=in_specs, out_specs=out_specs, check_vma=False
    )
```

time: 675 us -> 235 us (0.35)
  other arithmetic: 243 us -> 0.79 us
  local copies, waits for them, and re-layouts: 220 us -> 7.17 us
  waiting for transfers between devices: 25.8 us -> 74.4 us
  starting transfers between devices: 37.1 us -> 2.74 us
  Pallas kernels: 0 us -> 29.5 us
  between operations: 23.9 us -> 14.2 us
  matrix products: 10.1 us -> 1.53 us
    scatter-add x128 -> x0, other arithmetic: 215 us -> none
    scatter-add x192 -> x0, local copies, waits for them, and re-layouts: 100 us -> none
    gather x216 -> x0, local copies, waits for them, and re-layouts: 96.3 us -> none
    psum x0 -> x1, waiting for transfers between devices: none -> 74.4 us  [per_device(): lax.psum((grads, gproj_t, gtaps, gmix), everyone)]
    ppermute x18 -> x2, starting transfers between devices: 37 us -> 2.7 us  [the longest x1 2.25 us: per_device(): side = lax.ppermute(side, ('seq', 'chan'), moves)]
    pallas_call x0 -> x1, Pallas kernels: none -> 29.5 us  [per_device(): pl.pallas_call(band_kernel, out_shape=(jax.ShapeDtypeStruct((band_dev + H...]
    ppermute x18 -> x2, waiting for transfers between devices: 25.7 us -> 0.01 us  [the longest x1 0.01 us: per_device(): edge = lax.ppermute(edge, 'sub', [(0, 1), (1, 0)])]
    psum x5 -> x1, blocking collectives: 71.9 us -> 58.4 us  [per_device(): lax.psum((grads, gproj_t, gtaps, gmix), everyone)]
  transfers between devices with their start and end apart: 21 -> 3, of which waited for: 10 -> 1; matrix products, arithmetic and copies ran while one was open for 67% -> 2% of each run, Pallas kernels for 0% -> 0%
where the time goes in v1:
time: 235 us; the launch traced here: 234 us
  blocking collectives  104 us (44%)
  waiting for transfers between devices  74.4 us (32%)
  Pallas kernels  29.5 us (13%)
  between operations  14.2 us (6%)
  local copies, waits for them, and re-layouts  7.17 us (3%)
  starting transfers between devices  2.74 us (1%)
    psum x1, waiting for transfers between devices, per_device(): lax.psum((grads, gproj_t, gtaps, gmix), everyone)  74.4 us
    psum x1, blocking collectives, per_device(): lax.psum((grads, gproj_t, gtaps, gmix), everyone)  58.4 us
    pallas_call x1, Pallas kernels, per_device(): pl.pallas_call(band_kernel, out_shape=(jax.ShapeDtypeStruct((band_dev + H...  29.5 us
    all_gather x1, blocking collectives, per_device(): feats = lax.all_gather(features, ('seq', 'chan'), axis=0)  27.5 us
    unnamed x28, local copies, waits for them, and re-layouts  5.63 us
  transfers between devices with their start and end apart: 3, of which 1 were waited for; matrix products, arithmetic and copies ran while one was open for 2% of the time, Pallas kernels for 0%

profile of v1, /device:TPU:0, one launch (start us, length us, event | category | flops | bytes accessed | tf_op | source)
XLA Modules:
  0.0 233.9 jit_solution(9354067852330214430)
XLA Ops:
  7.2 0.0 copy-start.5
  7.2 0.0 all-reduce.4.cloned.1.call-start
  7.2 0.7 slice_select_fusion.1
  7.9 0.5 collective-permute-start
  8.4 0.0 copy-done.5
  8.4 27.5 %all-gather = bf16[1024,48]{0,1:T(8,128)(2,1)S(1)} all-gather(bf16[128,48]{0,1:T(8,128)(2,1)S(1)} %copy-done.5), channel_id=2, replica_groups=mesh['groups'=2,'seq'=4,'chan'=2,'sub'=2] {'seq','chan'}, dimensions={0}, use_global_device_ids=true | all-gather | bytes 110592 | tf_op jit(solution)/shard_map/all_gather | solution.py:281
  35.9 0.7 copy-done.8
  36.5 4.4 %all-gather.1 = bf16[2,48,32]{1,2,0:T(8,128)(2,1)S(1)} all-gather(bf16[1,48,32]{1,2,0:T(8,128)(2,1)S(1)} %bitcast.29), channel_id=1, replica_groups=mesh['groups'=2,'seq'=4,'chan'=2,'sub'=2] {'chan'}, dimensions={0}, use_global_device_ids=true | all-gather | bytes 9216 | tf_op jit(solution)/shard_map/all_gather | solution.py:284
  40.9 0.1 reshape.23
  41.0 0.1 copy.40.proj
  41.1 0.6 copy-done.7
  41.7 4.4 %all_gather.21 = bf16[2,32,32]{1,2,0:T(8,128)(2,1)S(1)} all-gather(bf16[2,32,16]{1,2,0:T(8,128)(2,1)S(1)} %copy-done.7), channel_id=1, replica_groups=mesh['groups'=2,'seq'=4,'chan'=2,'sub'=2] {'chan'}, dimensions={2}, use_global_device_ids=true | all-gather | bytes 6144 | tf_op jit(solution)/shard_map/all_gather | solution.py:285
  46.1 0.1 copy.41.mix
  46.3 0.0 copy-start.6
  46.3 0.0 copy-start.4
  46.3 0.1 copy.36
  46.4 0.5 copy-done.6
  47.0 0.1 copy.38
  47.1 0.0 collective-permute-done
  47.1 0.0 copy-done.4
  47.1 0.1 slice_select_fusion
  47.2 2.2 collective-permute-start.1
  49.4 0.0 copy-done.1
  49.4 0.0 copy-start.9
  49.4 0.1 copy.42.ro_col
  49.5 0.6 copy-done.9
  50.1 0.1 copy.39.pairs
  50.2 4.4 %all_gather.22.taps_in = f32[2,32,9]{2,1,0:T(8,128)S(1)} all-gather(f32[2,16,9]{2,1,0:T(8,128)S(1)} %copy.38), channel_id=1, replica_groups=mesh['groups'=2,'seq'=4,'chan'=2,'sub'=2] {'chan'}, dimensions={1}, use_global_device_ids=true | all-gather | bytes 3456 | tf_op jit(solution)/shard_map/all_gather | solution.py:286
  54.7 0.0 collective-permute-done.1
  54.7 0.1 concatenate.11
  54.8 0.0 copy-start
  54.8 0.1 constant_dynamic-slice_fusion.2.cot
  54.9 0.7 copy-done
  55.6 0.0 copy-done.2
  55.6 0.0 copy-done.3
  55.6 29.5 %shard_map.145 = (f32[72,128]{1,0:T(8,128)S(1)}, f32[4,32,128]{2,1,0:T(8,128)}, f32[4,32,128]{2,1,0:T(8,128)}, f32[32,96]{1,0:T(8,128)S(1)}, f32[2,32,9]{2,1,0:T(8,128)S(1)}, /*index=5*/f32[2,32,32]{2,1,0:T(8,128)S(1)}) custom-call(s32[2]{0:T(128)S(1)} %copy-done.2, s32[4]{0:T(128)S(1)} %copy-done.3, s32[4,2]{1,0:T(4,128)S(1)} %copy.39.pairs, ...), custom_call_target="tpu_custom_call" | custom-call | tf_op jit(solution)/shard_map/pallas_call | solution.py:312
  85.1 58.4 %all-reduce.1 = (f32[32,96]{1,0:T(8,128)S(1)}, f32[2,32,9]{2,1,0:T(8,128)S(1)}, f32[2,32,32]{2,1,0:T(8,128)S(1)}) all-reduce(f32[32,96]{1,0:T(8,128)S(1)} %get-tuple-element.15, f32[2,32,9]{2,1,0:T(8,128)S(1)} %get-tuple-element.16, ...), channel_id=1, replica_groups=mesh['groups'=2,'seq'=4,'chan'=2,'sub'=2] {'seq','chan','sub'}, use_global_device_ids=true, to_apply=%region_1.2 | all-reduce | flops 5696 | bytes 45568 | tf_op jit(solution)/shard_map/psum | solution.py:348
  143.5 0.1 constant_dynamic-slice_fusion
  143.6 0.0 all-reduce.4.cloned.1.call-update
  143.6 0.1 constant_dynamic-slice_fusion.3
  143.7 0.7 dynamic-slice_bitcast_fusion
  144.4 0.7 copy.46
  145.0 0.7 copy.45
  145.7 0.1 copy.43
  145.8 4.6 %all_gather.23 = f32[64,128]{0,1:T(8,128)S(1)} all-gather(f32[64,64]{0,1:T(8,128)S(1)} %copy.43), channel_id=1, replica_groups=mesh['groups'=2,'seq'=4,'chan'=2,'sub'=2] {'chan'}, dimensions={1}, use_global_device_ids=true | all-gather | bytes 49152 | tf_op jit(solution)/shard_map/all_gather | solution.py:360
  150.4 0.7 copy.44
  151.1 74.4 %all-reduce.4.cloned.1.call-done = f32[4,32,128]{2,1,0:T(8,128)} async-done(((f32[4,32,128]{2,1,0:T(8,128)}), f32[4,32,128]{2,1,0:T(8,128)}) %all-reduce.4.cloned.1.call-update) | async-done | bytes 65552 | tf_op jit(solution)/shard_map/psum | solution.py:348
  225.5 1.5 fusion
  (13 shorter events, 0.2 us)
Async XLA Ops:
  7.2 1.2 copy-start.5
  7.2 218.3 %all-reduce.4.cloned.1.call-start = ((), (), s32[]{:S(2)}) async-start(), calls=%async_computation | async-start | bytes 131072 | tf_op jit(solution)/shard_map/psum | solution.py:348
  7.9 39.1 %collective-permute-start = (f32[8,128]{1,0:T(8,128)S(1)}, f32[8,128]{1,0:T(8,128)S(1)}, u32[]{:S(2)}, u32[]{:S(2)}) collective-permute-start(f32[8,128]{1,0:T(8,128)S(1)} %slice_select_fusion.1), channel_id=1, source_target_pairs={{0,1},{1,0},{2,3},{3,2},{4,5},{5,4},{6,7},{7,6},{8,9},{9,8},{10,11... | collective-permute-start | bytes 12296 | tf_op jit(solution)/shard_map/ppermute | solution.py:288
  35.9 0.7 copy-start.8
  41.0 0.7 copy-start.7
  46.3 0.7 copy-start.6
  46.3 0.8 copy-start.4
  47.1 2.3 copy-start.1
  47.2 7.5 %collective-permute-start.1 = (f32[72,8]{1,0:T(8,128)S(1)}, f32[72,8]{1,0:T(8,128)S(1)}, u32[]{:S(2)}, u32[]{:S(2)}) collective-permute-start(f32[72,8]{1,0:T(8,128)S(1)} %slice_select_fusion), channel_id=1, source_target_pairs={{0,4},{6,2},{4,8},{10,6},{8,12},{14,10},{1,5},{7,3},{5,9},{11,7},{... | collective-permute-start | bytes 6920 | tf_op jit(solution)/shard_map/ppermute | solution.py:300
  49.4 0.7 copy-start.9
  54.8 0.8 copy-start
  54.9 0.7 copy-start.2
  54.9 0.7 copy-start.3
Sparse Core Ops, SparseCore 0:
  143.7 81.7 all-reduce.3

commit v2 on v1

--- a/solution.py
+++ b/solution.py
@@ -10,6 +10,7 @@
 GUARD = 32
 LOW = 16
 BATCH = 8
+MESH = pl.DeviceIdType.MESH
 EXACT = lax.Precision.HIGHEST
 NT = (((1,), (1,)), ((), ()))
 NN = (((1,), (0,)), ((), ()))
@@ -24,16 +25,165 @@
     return high, (value - high.astype(jnp.float32)).astype(jnp.bfloat16)
 
 
+def place():
+    return lax.axis_index("seq"), lax.axis_index("chan"), lax.axis_index("sub")
+
+
+def meet(sources, target_count):
+    barrier = pltpu.get_barrier_semaphore()
+    for device in sources:
+        pl.semaphore_signal(barrier, inc=1, device_id=device, device_id_type=MESH)
+    pl.semaphore_wait(barrier, target_count)
+
+
+def at(s, x, u):
+    return {"seq": s, "chan": x, "sub": u}
+
+
+def gather_kernel(
+    features, proj_t, mix, taps, cot,
+    feats, projs, mixes, taps_all, edge, side, side_edge,
+    send_feats, recv_feats, send_small, recv_small, send_cot, recv_cot,
+):
+    seq_count, chan_count = lax.axis_size("seq"), lax.axis_size("chan")
+    s, x, u = place()
+    bins = features.shape[0]
+    band = cot.shape[0]
+    peers, sources = [], []
+    for ds in range(seq_count):
+        for dx in range(chan_count):
+            if ds or dx:
+                peers.append(at(lax.rem(s + ds, seq_count), lax.rem(x + dx, chan_count), u))
+                back = (lax.rem(s + seq_count - ds, seq_count), lax.rem(x + chan_count - dx, chan_count))
+                sources.append(at(*back, u))
+    step = jnp.where(x == 0, 1, seq_count - 1)
+    ahead = lax.rem(s + step, seq_count)
+    behind = lax.rem(s + seq_count - step, seq_count)
+    other = 1 - u
+    meet(sources + [at(s, x, other), at(behind, x, other)], len(peers) + 2)
+
+    copies = []
+
+    def push(source, target, sems, j, device):
+        copy = pltpu.make_async_remote_copy(
+            src_ref=source, dst_ref=target, send_sem=sems[0].at[j], recv_sem=sems[1].at[j],
+            device_id=device, device_id_type=MESH,
+        )
+        copy.start()
+        copies.append(copy)
+
+    slot = pl.ds(pl.multiple_of((1 + s) * bins, bins), bins)
+    rim = pl.ds(pl.multiple_of((1 - u) * (band - HALO), HALO), HALO)
+    for j, device in enumerate(peers):
+        push(features, feats.at[x, slot], (send_feats, recv_feats), j, device)
+    push(cot, side, (send_cot, recv_cot), 0, at(ahead, x, u))
+    push(cot.at[rim], side_edge, (send_cot, recv_cot), 1, at(ahead, x, other))
+    push(cot.at[rim], edge, (send_cot, recv_cot), 2, at(s, x, other))
+    for dx in range(1, chan_count):
+        device = at(s, lax.rem(x + dx, chan_count), u)
+        small = (send_small, recv_small)
+        push(proj_t, projs.at[x], small, 3 * dx - 3, device)
+        push(mix, mixes.at[x], small, 3 * dx - 2, device)
+        push(taps, taps_all.at[x], small, 3 * dx - 1, device)
+    feats[x, slot] = features[...]
+    projs[x] = proj_t[...]
+    mixes[x] = mix[...]
+    taps_all[x] = taps[...]
+    for c in range(chan_count):
+        feats[c, :bins] = jnp.zeros((bins, features.shape[1]), features.dtype)
+        feats[c, (1 + seq_count) * bins :] = jnp.zeros((2 * bins, features.shape[1]), features.dtype)
+    for copy in copies:
+        copy.wait()
+
+
+def reduce_kernel(
+    part, misc, contact, proj_t,
+    contact_out, grad_features, grad_proj, grad_kernel, grad_mix,
+    parts, miscs, contacts, outgoing, arrived, taps_sum, send_a, recv_a, send_b, recv_b, send_c, recv_c,
+):
+    seq_count, chan_count = lax.axis_size("seq"), lax.axis_size("chan")
+    s, x, u = place()
+    layers, chan_dev = grad_kernel.shape[0], grad_kernel.shape[1]
+    width = proj_t.shape[1]
+    far = [lax.rem(s + j, seq_count) for j in range(1, seq_count)]
+    near = [(dx, du) for dx in range(chan_count) for du in range(2) if dx or du]
+
+    def neighbour(dx, du):
+        return lax.rem(x + dx, chan_count), lax.rem(u + du, 2)
+
+    everyone = [at(t, x, u) for t in far] + [at(s, *neighbour(dx, du)) for dx, du in near]
+    meet(everyone, len(everyone))
+    copies = []
+
+    def push(source, target, sems, j, device):
+        copy = pltpu.make_async_remote_copy(
+            src_ref=source, dst_ref=target, send_sem=sems[0].at[j], recv_sem=sems[1].at[j],
+            device_id=device, device_id_type=MESH,
+        )
+        copy.start()
+        return copy
+
+    first = []
+    for j, t in enumerate(far):
+        first.append(push(misc, miscs.at[s], (send_a, recv_a), 2 * j, at(t, x, u)))
+        first.append(push(part.at[t], parts.at[s], (send_a, recv_a), 2 * j + 1, at(t, x, u)))
+    shown = []
+    for dx in range(1, chan_count):
+        device = at(s, lax.rem(x + dx, chan_count), u)
+        shown.append(push(contact, contacts.at[x], (send_c, recv_c), dx - 1, device))
+    parts[s] = part[s]
+    miscs[s] = misc[...]
+    contacts[x] = contact[...]
+    for copy in first:
+        copy.wait()
+    f32 = jnp.float32
+    total = parts[0].astype(f32)
+    for t in range(1, seq_count):
+        total = total + parts[t].astype(f32)
+    for c in range(chan_count):
+        outgoing[c, 0] = total
+        rest = miscs[0, c].astype(f32)
+        for t in range(1, seq_count):
+            rest = rest + miscs[t, c].astype(f32)
+        outgoing[c, 1] = rest
+    second = []
+    for j, (dx, du) in enumerate(near):
+        nx, nu = neighbour(dx, du)
+        second.append(
+            push(outgoing.at[nx], arrived.at[2 * x + u], (send_b, recv_b), j, at(s, nx, nu))
+        )
+    arrived[2 * x + u] = outgoing[x]
+    for copy in shown:
+        copy.wait()
+    picture = contacts[0]
+    for c in range(1, chan_count):
+        picture = picture + contacts[c]
+    contact_out[...] = picture
+    for copy in second:
+        copy.wait()
+    total, rest = arrived[0, 0], arrived[0, 1]
+    for j in range(1, 2 * chan_count):
+        total, rest = total + arrived[j, 0], rest + arrived[j, 1]
+    grad_features[...] = mm(total.T, proj_t[...].astype(f32), NN, EXACT)
+    grad_proj[...] = rest.T[:width]
+    for l in range(layers):
+        grad_mix[l] = rest[:, width + l * chan_dev : width + (l + 1) * chan_dev]
+        off = width + layers * chan_dev + 9 * l
+        taps_sum[...] = rest
+        grad_kernel[l] = taps_sum[pl.ds(x * chan_dev, chan_dev), off : off + 9]
+
+
 def band_kernel(
-    dil, chroms, pairs, feats, proj, proj_t, mix, mix_t, taps_in, ro_col, ro_row, cot, tcot,
-    contact, maps, grads, gproj_t, gtaps, gmix,
-    taps, spread, env, prof, prof_t, x0, x1, h, go, gs, gf, go1, gs1, gpad, acc, spent,
+    dil, chroms, pairs, feats, projs, mixes, taps_in, ro_col, ro_row,
+    cot_own, cot_edge, cot_side, cot_side_edge, tcot,
+    contact, maps, part, misc,
+    taps, spread, env, prof, prof_t, x0, x1, h, go, gs, gf, go1, gs1, gpad, acc, spent, cot, picture, rest,
 ):
-    chans = proj.shape[1]
-    layers = mix.shape[0]
+    chans, width = projs.shape[1:]
+    layers, chan_dev = mixes.shape[1], mixes.shape[3]
     bin_dev = LANES
     seq_count, chan_count = lax.axis_size("seq"), lax.axis_size("chan")
-    seq_pos, chan_pos, sub_pos = lax.axis_index("seq"), lax.axis_index("chan"), lax.axis_index("sub")
+    seq_pos, chan_pos, sub_pos = place()
     total = seq_count * bin_dev
     own_bins = bin_dev // chan_count
     rows = h.shape[1]
@@ -70,18 +220,42 @@
     c_w = lax.broadcasted_iota(jnp.int32, (wide, wide), 1) // chans
     diag = r_w == c_w
     for l in range(layers):
-        for side, source in enumerate((mix_t, mix)):
-            tall = mm(fan, source[l]).astype(jnp.bfloat16)
+        mixed = jnp.concatenate([mixes[c, l] for c in range(chan_count)], axis=1)
+        for side, dims in enumerate((NT, NN)):
+            tall = mm(fan, mixed, dims).astype(jnp.bfloat16)
             full = mm(tall, fan, NT)
             spread[2 * l + side] = jnp.where(diag, full, 0.0).astype(jnp.bfloat16)
         for t in range(9):
-            taps[l, t] = jnp.broadcast_to(taps_in[l][:, t : t + 1], (chans, LANES))
-
-    prof[...] = mm(feats[pl.ds(LANES, total), :], proj[...])
+            for c in range(chan_count):
+                column = taps_in[c, l][:, t : t + 1]
+                taps[l, t, c * chan_dev : (c + 1) * chan_dev, :] = jnp.broadcast_to(
+                    column, (chan_dev, LANES)
+                )
+
+    turn = lax.rem(LANES + GUARD - chan_pos * own_bins, LANES)
+    column = lane - GUARD + chan_pos * own_bins
+    inside = (column >= 0) & (column < LANES)
+    own_at = pl.multiple_of(sub_pos * HALO, HALO)
+    lines = [
+        jnp.where(inside, pltpu.roll(here[...], turn, 1), pltpu.roll(there[...], turn, 1))
+        for here, there in ((cot_own, cot_side), (cot_edge, cot_side_edge))
+    ]
+    cot[...] = jnp.where(
+        sub_pos == 0,
+        jnp.concatenate(lines, axis=0),
+        jnp.concatenate(lines[::-1], axis=0),
+    )
+
+    def project(rows_at, count):
+        sums = [mm(projs[c], feats[c, pl.ds(rows_at, count), :], NT) for c in range(chan_count)]
+        return sum(sums[1:], sums[0])
+
     for b in range(seq_count):
-        prof_t[b] = mm(proj_t[...], feats[(b + 1) * LANES : (b + 2) * LANES, :], NT)
-    start = pl.multiple_of(first + LANES, 16)
-    env[...] = mm(proj_t[...], feats[pl.ds(start, 2 * LANES), :], NT)
+        block = [feats[c, (b + 1) * LANES : (b + 2) * LANES, :] for c in range(chan_count)]
+        sums = [mm(block[c], projs[c], NT) for c in range(chan_count)]
+        prof[b * LANES : (b + 1) * LANES, :] = sum(sums[1:], sums[0])
+        prof_t[b] = project((b + 1) * LANES, LANES)
+    env[...] = project(pl.multiple_of(first + LANES, 16), 2 * LANES)
     ro = jnp.broadcast_to(ro_col[...], (chans, LANES))
 
     for buf in (x0, x1, gs, gs1):
@@ -133,10 +307,15 @@
                 if l + 1 < layers:
                     xs[l + 1][LOW + r0 + j] = new
                 else:
-                    contact[pl.ds(i * BATCH + j, 1), :] = jnp.sum(new * ro, axis=0, keepdims=True)
+                    picture[pl.ds(i * BATCH + j, 1), :] = jnp.sum(new * ro, axis=0, keepdims=True)
             return 0
 
         lax.fori_loop(0, (rows - HALO * (l + 1)) // BATCH, layer, 0)
+
+    shown = picture[pl.ds(own_at, own_rows), :] * own_lane
+    contact[...] = pltpu.roll(shown, lax.rem(LANES - turn, LANES), 1)
+    for c in range(chan_count):
+        rest[c] = jnp.zeros((chans, LANES), jnp.float32)
 
     def pull(l, r0, source, target):
         g = source[pl.ds(r0, BATCH)].reshape(wide, LANES)
@@ -164,10 +343,17 @@
 
         zero = jnp.zeros((chans, LANES), jnp.float32)
         sums = lax.fori_loop(0, own_rows // BATCH, body, (zero,) * 9)
+        tile = jnp.zeros((chans, LANES), jnp.float32)
         for t in range(9):
-            gtaps[l, :, t : t + 1] = jnp.sum(sums[t], axis=1, keepdims=True)
+            line = jnp.sum(sums[t], axis=1, keepdims=True)
+            off = width + layers * chan_dev + 9 * l + t
+            tile = tile + jnp.where(lane == off, line, 0.0)
         tall = jnp.sum(jnp.where(diag, acc[...], 0.0).reshape(BATCH, chans, wide), axis=0)
-        gmix[l] = mm(tall, fan.astype(jnp.float32), precision=EXACT)
+        row_e = lax.rem(lax.broadcasted_iota(jnp.int32, (wide, LANES), 0), chans)
+        col_e = lax.broadcasted_iota(jnp.int32, (wide, LANES), 1) - width - l * chan_dev
+        for c in range(chan_count):
+            hit = (col_e >= 0) & (col_e < chan_dev) & (row_e == col_e + c * chan_dev)
+            rest[c] = rest[c] + tile + mm(tall, hit.astype(jnp.float32), precision=EXACT)
 
     def last_out(i, _):
         r0 = sub_pos * 2 * HALO + i * BATCH
@@ -230,9 +416,9 @@
     near = far[:, :LANES] + near
     zero = jnp.zeros((chans, LANES), jnp.float32)
     whole = jnp.concatenate([near, far[:, LANES:], zero], axis=1)
-    place = first + LANES
-    tile = place // LANES
-    whole = pltpu.roll(whole, lax.rem(place, LANES), 1)
+    corner = first + LANES
+    tile = corner // LANES
+    whole = pltpu.roll(whole, lax.rem(corner, LANES), 1)
     for b in range(gpad.shape[0]):
         gpad[b] = zero
     for b in range(3):
@@ -255,81 +441,80 @@
         gpad[1 + p] = gpad[1 + p] + to_first
         gpad[1 + q] = gpad[1 + q] + to_second
 
-    total_proj = jnp.zeros(gproj_t.shape, jnp.float32)
+    pieces = []
     for b in range(seq_count):
-        g = gpad[1 + b]
-        grads[b] = g
-        high, low = split(g)
-        block = feats[(b + 1) * LANES : (b + 2) * LANES, :]
-        total_proj = total_proj + mm(high, block) + mm(low, block)
-    gproj_t[...] = total_proj
+        part[b] = gpad[1 + b].astype(jnp.bfloat16)
+        pieces.append(split(gpad[1 + b]))
+    for c in range(chan_count):
+        total_proj = jnp.zeros((chans, width), jnp.float32)
+        for b in range(seq_count):
+            block = feats[c, (b + 1) * LANES : (b + 2) * LANES, :]
+            total_proj = total_proj + mm(pieces[b][0], block) + mm(pieces[b][1], block)
+        blank = jnp.zeros((chans, LANES - width), jnp.float32)
+        misc[c] = (rest[c] + jnp.concatenate([total_proj, blank], axis=1)).astype(jnp.bfloat16)
 
 
 def per_device(
     features, proj, kernel, mix, readout, dilations, chrom_lengths, pairs, contact_cot, trans_cot
 ):
-    bin_dev = features.shape[0]
+    f32, bf16 = jnp.float32, jnp.bfloat16
+    bin_dev, width = features.shape
     chans = proj.shape[1]
     band_dev = contact_cot.shape[0]
-    layers = kernel.shape[0]
+    layers, chan_dev = kernel.shape[:2]
     seq_count, chan_count = lax.axis_size("seq"), lax.axis_size("chan")
-    seq_pos, chan_pos, sub_pos = lax.axis_index("seq"), lax.axis_index("chan"), lax.axis_index("sub")
-    own_bins = bin_dev // chan_count
     total = bin_dev * seq_count
     rows = band_dev + 3 * HALO
-
-    feats = lax.all_gather(features, ("seq", "chan"), axis=0)
-    feats = feats.reshape(seq_count, chan_count, bin_dev, -1).transpose(0, 2, 1, 3)
-    feats = jnp.pad(feats.reshape(total, -1), ((bin_dev, 2 * bin_dev), (0, 0)))
-    proj_all = lax.all_gather(proj, "chan", axis=0, tiled=True)
-    mix_all = lax.all_gather(mix, "chan", axis=2, tiled=True)
-    taps = lax.all_gather(kernel, "chan", axis=1, tiled=True)
-    edge = jnp.where(sub_pos == 0, contact_cot[-HALO:], contact_cot[:HALO])
-    edge = lax.ppermute(edge, "sub", [(0, 1), (1, 0)])
-    zeros = jnp.zeros_like(edge)
-    cot = jnp.where(
-        sub_pos == 0,
-        jnp.concatenate([contact_cot, edge], axis=0),
-        jnp.concatenate([edge, contact_cot], axis=0),
-    )
-    side = jnp.where(chan_pos == 0, cot[:, -HALO:], cot[:, :HALO])
-    moves = []
-    for s in range(seq_count - 1):
-        moves.append((s * chan_count, (s + 1) * chan_count))
-        moves.append(((s + 2) * chan_count - 1, (s + 1) * chan_count - 1))
-    side = lax.ppermute(side, ("seq", "chan"), moves)
-    blank = jnp.zeros((cot.shape[0], GUARD - HALO), jnp.float32)
-    cot = jnp.concatenate([blank, side, cot, side, blank], axis=1)
-    cot = lax.dynamic_slice_in_dim(cot, chan_pos * own_bins, LANES, 1)
-
-    f32 = jnp.float32
     smem = pl.BlockSpec(memory_space=pltpu.SMEM)
     vmem = pl.BlockSpec(memory_space=pltpu.VMEM)
+    shape = jax.ShapeDtypeStruct
+    proj_t = proj.T
+
+    def sems(count):
+        return [pltpu.SemaphoreType.DMA((count,))] * 2
+
+    gathered = pl.pallas_call(
+        gather_kernel,
+        out_shape=(
+            shape((chan_count, (seq_count + 3) * bin_dev, width), bf16),
+            shape((chan_count, chans, width), bf16),
+            shape((chan_count, layers, chans, chan_dev), bf16),
+            shape((chan_count, layers, chan_dev, 9), f32),
+            shape((HALO, bin_dev), f32),
+            shape((band_dev, bin_dev), f32),
+            shape((HALO, bin_dev), f32),
+        ),
+        in_specs=[vmem] * 5,
+        out_specs=(vmem,) * 7,
+        scratch_shapes=[
+            *sems(seq_count * chan_count - 1), *sems(3 * (chan_count - 1)), *sems(3)
+        ],
+        compiler_params=pltpu.CompilerParams(collective_id=0, has_side_effects=True),
+    )(features, proj_t, mix, kernel, contact_cot)
+    feats, projs, mixes, taps, edge, side, side_edge = gathered
+
     field = pltpu.VMEM((2 * LOW + rows, chans, LANES), f32)
     plain = pltpu.VMEM((rows, chans, LANES), f32)
     wide = BATCH * chans
-    width = proj_all.shape[0]
-    contact, maps, grads, gproj_t, gtaps, gmix = pl.pallas_call(
+    contact, maps, part, misc = pl.pallas_call(
         band_kernel,
         out_shape=(
-            jax.ShapeDtypeStruct((band_dev + HALO, LANES), f32),
-            jax.ShapeDtypeStruct(trans_cot.shape, f32),
-            jax.ShapeDtypeStruct((seq_count, chans, LANES), f32),
-            jax.ShapeDtypeStruct((chans, width), f32),
-            jax.ShapeDtypeStruct((layers, chans, 9), f32),
-            jax.ShapeDtypeStruct((layers, chans, chans), f32),
+            shape((band_dev, LANES), f32),
+            shape(trans_cot.shape, f32),
+            shape((seq_count, chans, LANES), bf16),
+            shape((chan_count, chans, LANES), bf16),
         ),
-        in_specs=[smem] * 3 + [vmem] * 10,
-        out_specs=(vmem,) * 6,
+        in_specs=[smem] * 3 + [vmem] * 11,
+        out_specs=(vmem,) * 4,
         scratch_shapes=[
             pltpu.VMEM((layers, 9, chans, LANES), f32),
-            pltpu.VMEM((2 * layers, wide, wide), jnp.bfloat16),
+            pltpu.VMEM((2 * layers, wide, wide), bf16),
             pltpu.VMEM((chans, 2 * LANES), f32),
             pltpu.VMEM((total, chans), f32),
             pltpu.VMEM((seq_count, chans, LANES), f32),
             field,
             field,
-            pltpu.VMEM((layers, rows, chans, LANES), jnp.bfloat16),
+            pltpu.VMEM((layers, rows, chans, LANES), bf16),
             plain,
             field,
             plain,
@@ -338,26 +523,37 @@
             pltpu.VMEM((seq_count + 3, chans, LANES), f32),
             pltpu.VMEM((wide, wide), f32),
             pltpu.VMEM((LANES, LANES), f32),
+            pltpu.VMEM((band_dev + HALO, LANES), f32),
+            pltpu.VMEM((band_dev + HALO, LANES), f32),
+            pltpu.VMEM((chan_count, chans, LANES), f32),
         ],
         compiler_params=pltpu.CompilerParams(vmem_limit_bytes=48 * 1024 * 1024),
     )(
-        dilations, chrom_lengths, pairs, feats, proj_all, proj_all.T, mix_all,
-        mix_all.transpose(0, 2, 1), taps, readout[:, None], readout[None, :], cot, trans_cot,
+        dilations, chrom_lengths, pairs, feats, projs, mixes, taps,
+        readout[:, None], readout[None, :], contact_cot, edge, side, side_edge, trans_cot,
     )
-    everyone = ("seq", "chan", "sub")
-    grads, gproj_t, gtaps, gmix = lax.psum((grads, gproj_t, gtaps, gmix), everyone)
-    own = lax.dynamic_index_in_dim(grads, seq_pos, 0, keepdims=False)
-    grad_features = lax.dot_general(
-        own, proj.astype(f32), (((0,), (1,)), ((), ())), precision=EXACT
-    )
-    chan_dev, width_dev = kernel.shape[1], proj.shape[0]
-    grad_proj = lax.dynamic_slice_in_dim(gproj_t, chan_pos * width_dev, width_dev, 1).T
-    grad_kernel = lax.dynamic_slice_in_dim(gtaps, chan_pos * chan_dev, chan_dev, 1)
-    grad_mix = lax.dynamic_slice_in_dim(gmix, chan_pos * chan_dev, chan_dev, 2)
-    contact = lax.dynamic_slice(
-        contact, (sub_pos * HALO, jnp.int32(GUARD)), (band_dev, own_bins)
-    )
-    contact = lax.all_gather(contact, "chan", axis=1, tiled=True)
+    contact, grad_features, grad_proj, grad_kernel, grad_mix = pl.pallas_call(
+        reduce_kernel,
+        out_shape=(
+            shape((band_dev, LANES), f32),
+            shape((bin_dev, width), f32),
+            shape((width, chans), f32),
+            shape((layers, chan_dev, 9), f32),
+            shape((layers, chans, chan_dev), f32),
+        ),
+        in_specs=[vmem] * 4,
+        out_specs=(vmem,) * 5,
+        scratch_shapes=[
+            pltpu.VMEM((seq_count, chans, LANES), bf16),
+            pltpu.VMEM((seq_count, chan_count, chans, LANES), bf16),
+            pltpu.VMEM((chan_count, band_dev, LANES), f32),
+            pltpu.VMEM((chan_count, 2, chans, LANES), f32),
+            pltpu.VMEM((2 * chan_count, 2, chans, LANES), f32),
+            pltpu.VMEM((chans, LANES), f32),
+            *sems(2 * (seq_count - 1)), *sems(2 * chan_count - 1), *sems(chan_count - 1),
+        ],
+        compiler_params=pltpu.CompilerParams(collective_id=1, has_side_effects=True),
+    )(part, misc, contact, proj_t)
     return (contact, maps, grad_features, grad_proj, grad_kernel, grad_mix)
 
 

time: 235 us -> 72.6 us (0.31)
  blocking collectives: 104 us -> 0 us
  waiting for transfers between devices: 74.4 us -> 0 us
  Pallas kernels: 29.5 us -> 54.6 us
  between operations: 14.2 us -> 0.73 us
  local copies, waits for them, and re-layouts: 7.17 us -> 16.4 us
  starting transfers between devices: 2.74 us -> 0 us
    psum x1 -> x0, waiting for transfers between devices: 74.4 us -> none  [per_device(): lax.psum((grads, gproj_t, gtaps, gmix), everyone)]
    psum x1 -> x0, blocking collectives: 58.4 us -> none  [per_device(): lax.psum((grads, gproj_t, gtaps, gmix), everyone)]
    all_gather x5 -> x0, blocking collectives: 45.2 us -> none  [the longest x1 27.5 us: per_device(): feats = lax.all_gather(features, ('seq', 'chan'), axis=0)]
    pallas_call x1 -> x3, Pallas kernels: 29.5 us -> 54.6 us  [the longest x1 29.2 us: per_device(): pl.pallas_call(band_kernel, out_shape=(shape((band_dev, LANES), f32), sha...]
    unnamed x28 -> x49, local copies, waits for them, and re-layouts: 5.63 us -> 16.3 us
    ppermute x2 -> x0, starting transfers between devices: 2.7 us -> none  [the longest x1 2.25 us: per_device(): side = lax.ppermute(side, ('seq', 'chan'), moves)]
  transfers between devices with their start and end apart: 3 -> 0, of which waited for: 1 -> 0; matrix products, arithmetic and copies ran while one was open for 2% -> 0% of each run, Pallas kernels for 0% -> 0%
where the time goes in v2:
time: 72.6 us; the launch traced here: 71.7 us
  Pallas kernels  54.6 us (75%)
  local copies, waits for them, and re-layouts  16.4 us (23%)
  between operations  0.73 us (1%)
    pallas_call x1, Pallas kernels, per_device(): pl.pallas_call(band_kernel, out_shape=(shape((band_dev, LANES), f32), sha...  29.2 us
    unnamed x49, local copies, waits for them, and re-layouts  16.3 us
    pallas_call x1, Pallas kernels, per_device(): pl.pallas_call(gather_kernel, out_shape=(shape((chan_count, (seq_count +...  14 us
    pallas_call x1, Pallas kernels, per_device(): pl.pallas_call(reduce_kernel, out_shape=(shape((band_dev, LANES), f32), s...  11.5 us

profile of v2, /device:TPU:0, one launch (start us, length us, event | category | flops | bytes accessed | tf_op | source)
XLA Modules:
  0.0 71.7 jit_solution(7962510007680689690)
XLA Ops:
  0.6 0.0 copy-start.19
  0.6 0.7 copy-done.19
  1.3 0.1 copy.19.pairs
  1.4 0.0 copy-start.18
  1.4 1.4 %copy.18.taps = f32[2,16,9]{2,1,0:T(8,128)} copy(f32[2,16,9]{1,0,2:T(2,128)} %param.12) | data formatting | bytes 2304 | tf_op args[2]
  2.8 0.0 copy-done.18
  2.8 0.0 copy-start.12
  2.8 0.7 copy.17.mix
  3.5 0.0 copy-done.12
  3.5 0.0 copy-start.17
  3.5 0.1 copy.20.ro_col
  3.6 0.6 copy-done.17
  4.2 0.7 %copy.16.features = bf16[128,48]{1,0:T(8,128)(2,1)} copy(bf16[128,48]{0,1:T(8,128)(2,1)S(1)} %copy-done.17) | data formatting | bytes 24576 | tf_op args[0]
  4.9 0.0 copy-start.1
  4.9 0.0 copy-start.2
  4.9 14.0 %shard_map.145 = (bf16[2,896,48]{2,1,0:T(8,128)(2,1)}, bf16[2,32,48]{2,1,0:T(8,128)(2,1)}, bf16[2,2,32,16]{3,2,1,0:T(8,128)(2,1)}, f32[2,2,16,9]{3,2,1,0:T(8,128...) custom-call(bf16[128,48]{1,0:T(8,128)(2,1)} %copy.16.features, bf16[32,48]{1,0:T(8,128)(2,1)} %bitcast.5, ...), custom_call_target="tpu_custom_call" | custom-call | tf_op jit(solution)/shard_map/pallas_call | solution.py:476
  18.9 0.0 copy-start.11
  18.9 0.0 copy-start.10
  18.9 0.0 copy-start.13
  18.9 0.0 copy-start.14
  18.9 0.0 copy-done.1
  19.0 0.0 copy-done.2
  19.0 0.6 copy-done.11
  19.6 0.0 copy-done.10
  19.6 0.0 copy-done.13
  19.6 0.0 copy-done.14
  19.6 0.0 copy-start
  19.6 1.0 %copy-done = bf16[2,896,48]{2,1,0:T(8,128)(2,1)S(1)} copy-done((bf16[2,896,48]{2,1,0:T(8,128)(2,1)S(1)}, bf16[2,896,48]{2,1,0:T(8,128)(2,1)}, u32[]{:S(2)}) %copy-start) | copy-done | bytes 172056
  20.6 0.0 copy-start.3
  20.6 0.8 %copy-done.3 = bf16[2,2,32,16]{3,2,1,0:T(8,128)(2,1)S(1)} copy-done((bf16[2,2,32,16]{3,2,1,0:T(8,128)(2,1)S(1)}, bf16[2,2,32,16]{3,2,1,0:T(8,128)(2,1)}, u32[]{:S(2)}) %copy-start.3) | copy-done | bytes 4120
  21.4 0.0 copy-start.4
  21.4 0.8 %copy-done.4 = f32[2,2,16,9]{3,2,1,0:T(8,128)S(1)} copy-done((f32[2,2,16,9]{3,2,1,0:T(8,128)S(1)}, f32[2,2,16,9]{3,2,1,0:T(8,128)}, u32[]{:S(2)}) %copy-start.4) | copy-done | bytes 2328
  22.1 0.0 copy-start.5
  22.1 0.8 %copy-done.5 = f32[64,128]{1,0:T(8,128)S(1)} copy-done((f32[64,128]{1,0:T(8,128)S(1)}, f32[64,128]{1,0:T(8,128)}, u32[]{:S(2)}) %copy-start.5) | copy-done | bytes 32792
  22.9 0.7 copy-done.8
  23.6 29.2 %shard_map.146 = (f32[64,128]{1,0:T(8,128)S(1)}, f32[4,32,128]{2,1,0:T(8,128)}, bf16[4,32,128]{2,1,0:T(8,128)(2,1)S(1)}, bf16[2,32,128]{2,1,0:T(8,128)(2,1)S(1)}) custom-call(s32[2]{0:T(128)S(1)} %copy-done.13, s32[4]{0:T(128)S(1)} %copy-done.14, s32[4,2]{1,0:T(4,128)S(1)} %copy.19.pairs, bf16[2,896,48]{2,1,0:T(8,128)(2,1)S(1)} %copy-done, ...), custom_call_target="tpu_custom_call" | custom-call | tf_op jit(solution)/shard_map/pallas_call | solution.py:499
  52.8 0.6 copy-done.6
  53.4 0.6 copy-done.7
  54.0 0.6 copy-done.9
  54.6 11.5 %shard_map.147 = (f32[64,128]{1,0:T(8,128)}, f32[128,48]{1,0:T(8,128)}, f32[48,32]{1,0:T(8,128)}, f32[2,16,9]{2,1,0:T(8,128)}, f32[2,32,16]{2,1,0:T(8,128)}) custom-call(bf16[4,32,128]{2,1,0:T(8,128)(2,1)} %copy-done.7, bf16[2,32,128]{2,1,0:T(8,128)(2,1)} %copy-done.9, f32[64,128]{1,0:T(8,128)} %copy-done.6, bf16[32,48]{1,0:T(8,128)(2,1)} %bitcast.6), custom_call_target="tpu_custom_call" | custom-call | tf_op jit(solution)/shard_map/pallas_call | solution.py:535
  66.1 0.0 copy-start.15
  66.1 1.4 %copy.23 = f32[2,16,9]{1,0,2:T(2,128)} copy(f32[2,16,9]{2,1,0:T(8,128)} %get-tuple-element.42) | data formatting | bytes 2304
  67.5 1.4 %copy.22 = f32[48,32]{0,1:T(8,128)} copy(f32[48,32]{1,0:T(8,128)} %get-tuple-element.41) | data formatting | bytes 12288
  68.9 1.4 %copy.24 = f32[2,32,16]{1,2,0:T(8,128)} copy(f32[2,32,16]{2,1,0:T(8,128)} %get-tuple-element.43) | data formatting | bytes 8192
  70.4 0.0 copy-done.15
  70.4 0.7 copy.21
  71.1 0.1 copy-done.16
  71.1 0.6 copy.26
  (5 shorter events, 0.0 us)
Async XLA Ops:
  0.6 0.7 copy-start.19
  1.4 1.4 %copy-start.18 = (bf16[2,32,16]{1,2,0:T(8,128)(2,1)S(1)}, bf16[2,32,16]{1,2,0:T(8,128)(2,1)}, u32[]{:S(2)}) copy-start(bf16[2,32,16]{1,2,0:T(8,128)(2,1)} %param.13) | copy-start | bytes 6148
  2.8 0.7 copy-start.12
  3.5 0.7 copy-start.17
  4.9 14.0 %copy-start.1 = (f32[64,128]{1,0:T(8,128)S(1)}, f32[64,128]{1,0:T(8,128)}, u32[]{:S(2)}) copy-start(f32[64,128]{1,0:T(8,128)} %cot_own.1) | copy-start | bytes 98308
  4.9 14.0 %copy-start.2 = (f32[4,32,128]{2,1,0:T(8,128)S(1)}, f32[4,32,128]{2,1,0:T(8,128)}, u32[]{:S(2)}) copy-start(f32[4,32,128]{2,1,0:T(8,128)} %tcot.1) | copy-start | bytes 196612
  18.9 0.7 copy-start.11
  18.9 0.7 copy-start.10
  18.9 0.7 copy-start.13
  18.9 0.7 copy-start.14
  19.6 1.0 %copy-start = (bf16[2,896,48]{2,1,0:T(8,128)(2,1)S(1)}, bf16[2,896,48]{2,1,0:T(8,128)(2,1)}, u32[]{:S(2)}) copy-start(bf16[2,896,48]{2,1,0:T(8,128)(2,1)} %get-tuple-element.22.feats) | copy-start | bytes 516100
  20.6 0.8 %copy-start.3 = (bf16[2,2,32,16]{3,2,1,0:T(8,128)(2,1)S(1)}, bf16[2,2,32,16]{3,2,1,0:T(8,128)(2,1)}, u32[]{:S(2)}) copy-start(bf16[2,2,32,16]{3,2,1,0:T(8,128)(2,1)} %get-tuple-element.24.mixes) | copy-start | bytes 12292
  21.4 0.8 %copy-start.4 = (f32[2,2,16,9]{3,2,1,0:T(8,128)S(1)}, f32[2,2,16,9]{3,2,1,0:T(8,128)}, u32[]{:S(2)}) copy-start(f32[2,2,16,9]{3,2,1,0:T(8,128)} %get-tuple-element.25.taps_in) | copy-start | bytes 6916
  22.1 0.8 %copy-start.5 = (f32[64,128]{1,0:T(8,128)S(1)}, f32[64,128]{1,0:T(8,128)}, u32[]{:S(2)}) copy-start(f32[64,128]{1,0:T(8,128)} %get-tuple-element.27.cot_side) | copy-start | bytes 98308
  22.9 0.7 copy-start.8
  52.8 0.6 copy-start.6
  53.4 0.6 copy-start.7
  54.0 0.6 copy-start.9
  66.1 4.3 %copy-start.15 = (f32[128,48]{1,0:T(8,128)S(1)}, f32[128,48]{1,0:T(8,128)}, u32[]{:S(2)}) copy-start(f32[128,48]{1,0:T(8,128)} %get-tuple-element.40) | copy-start | bytes 73732
  70.4 0.8 %copy-start.16 = (f32[64,128]{1,0:T(8,128)S(1)}, f32[64,128]{1,0:T(8,128)}, u32[]{:S(2)}) copy-start(f32[64,128]{1,0:T(8,128)} %get-tuple-element.50) | copy-start | bytes 98308

commit v3 on v2

--- a/solution.py
+++ b/solution.py
@@ -47,7 +47,6 @@
 ):
     seq_count, chan_count = lax.axis_size("seq"), lax.axis_size("chan")
     s, x, u = place()
-    bins = features.shape[0]
     band = cot.shape[0]
     peers, sources = [], []
     for ds in range(seq_count):
@@ -72,10 +71,9 @@
         copy.start()
         copies.append(copy)
 
-    slot = pl.ds(pl.multiple_of((1 + s) * bins, bins), bins)
     rim = pl.ds(pl.multiple_of((1 - u) * (band - HALO), HALO), HALO)
     for j, device in enumerate(peers):
-        push(features, feats.at[x, slot], (send_feats, recv_feats), j, device)
+        push(features, feats.at[x, s], (send_feats, recv_feats), j, device)
     push(cot, side, (send_cot, recv_cot), 0, at(ahead, x, u))
     push(cot.at[rim], side_edge, (send_cot, recv_cot), 1, at(ahead, x, other))
     push(cot.at[rim], edge, (send_cot, recv_cot), 2, at(s, x, other))
@@ -85,13 +83,10 @@
         push(proj_t, projs.at[x], small, 3 * dx - 3, device)
         push(mix, mixes.at[x], small, 3 * dx - 2, device)
         push(taps, taps_all.at[x], small, 3 * dx - 1, device)
-    feats[x, slot] = features[...]
+    feats[x, s] = features[...]
     projs[x] = proj_t[...]
     mixes[x] = mix[...]
     taps_all[x] = taps[...]
-    for c in range(chan_count):
-        feats[c, :bins] = jnp.zeros((bins, features.shape[1]), features.dtype)
-        feats[c, (1 + seq_count) * bins :] = jnp.zeros((2 * bins, features.shape[1]), features.dtype)
     for copy in copies:
         copy.wait()
 
@@ -104,7 +99,7 @@
     seq_count, chan_count = lax.axis_size("seq"), lax.axis_size("chan")
     s, x, u = place()
     layers, chan_dev = grad_kernel.shape[0], grad_kernel.shape[1]
-    width = proj_t.shape[1]
+    chans, width = proj_t.shape
     far = [lax.rem(s + j, seq_count) for j in range(1, seq_count)]
     near = [(dx, du) for dx in range(chan_count) for du in range(2) if dx or du]
 
@@ -164,10 +159,13 @@
     total, rest = arrived[0, 0], arrived[0, 1]
     for j in range(1, 2 * chan_count):
         total, rest = total + arrived[j, 0], rest + arrived[j, 1]
-    grad_features[...] = mm(total.T, proj_t[...].astype(f32), NN, EXACT)
-    grad_proj[...] = rest.T[:width]
+    blank = jnp.zeros((chans, LANES - width), f32)
+    proj = jnp.concatenate([proj_t[...].astype(f32), blank], axis=1).T[:width]
+    grad_features[...] = mm(proj, total, NN, EXACT)
+    grad_proj[...] = rest[:, :width]
+    flipped = rest.T
     for l in range(layers):
-        grad_mix[l] = rest[:, width + l * chan_dev : width + (l + 1) * chan_dev]
+        grad_mix[l] = flipped[width + l * chan_dev : width + (l + 1) * chan_dev]
         off = width + layers * chan_dev + 9 * l
         taps_sum[...] = rest
         grad_kernel[l] = taps_sum[pl.ds(x * chan_dev, chan_dev), off : off + 9]
@@ -177,10 +175,10 @@
     dil, chroms, pairs, feats, projs, mixes, taps_in, ro_col, ro_row,
     cot_own, cot_edge, cot_side, cot_side_edge, tcot,
     contact, maps, part, misc,
-    taps, spread, env, prof, prof_t, x0, x1, h, go, gs, gf, go1, gs1, gpad, acc, spent, cot, picture, rest,
+    taps, spread, env, prof, prof_t, x0, x1, h, go, gs, gf, go1, gs1, gpad, acc, spent, cot, picture, rest, mixed_t,
 ):
     chans, width = projs.shape[1:]
-    layers, chan_dev = mixes.shape[1], mixes.shape[3]
+    layers, chan_dev = mixes.shape[1], mixes.shape[2]
     bin_dev = LANES
     seq_count, chan_count = lax.axis_size("seq"), lax.axis_size("chan")
     seq_pos, chan_pos, sub_pos = place()
@@ -220,8 +218,10 @@
     c_w = lax.broadcasted_iota(jnp.int32, (wide, wide), 1) // chans
     diag = r_w == c_w
     for l in range(layers):
-        mixed = jnp.concatenate([mixes[c, l] for c in range(chan_count)], axis=1)
-        for side, dims in enumerate((NT, NN)):
+        for c in range(chan_count):
+            mixed_t[c * chan_dev : (c + 1) * chan_dev, :] = mixes[c, l].astype(jnp.float32)
+        mixed = mixed_t[...].astype(jnp.bfloat16)
+        for side, dims in enumerate((NN, NT)):
             tall = mm(fan, mixed, dims).astype(jnp.bfloat16)
             full = mm(tall, fan, NT)
             spread[2 * l + side] = jnp.where(diag, full, 0.0).astype(jnp.bfloat16)
@@ -246,16 +246,18 @@
         jnp.concatenate(lines[::-1], axis=0),
     )
 
-    def project(rows_at, count):
-        sums = [mm(projs[c], feats[c, pl.ds(rows_at, count), :], NT) for c in range(chan_count)]
-        return sum(sums[1:], sums[0])
-
+    zero = jnp.zeros((chans, LANES), jnp.float32)
+    for b in (0, seq_count + 1, seq_count + 2):
+        prof_t[b] = zero
     for b in range(seq_count):
-        block = [feats[c, (b + 1) * LANES : (b + 2) * LANES, :] for c in range(chan_count)]
-        sums = [mm(block[c], projs[c], NT) for c in range(chan_count)]
-        prof[b * LANES : (b + 1) * LANES, :] = sum(sums[1:], sums[0])
-        prof_t[b] = project((b + 1) * LANES, LANES)
-    env[...] = project(pl.multiple_of(first + LANES, 16), 2 * LANES)
+        sums = [mm(projs[c], feats[c, b]) for c in range(chan_count)]
+        block = sum(sums[1:], sums[0])
+        prof_t[1 + b] = block
+        prof[b * LANES : (b + 1) * LANES, :] = block.T
+    corner = first + LANES
+    tile, lead = corner // LANES, lax.rem(corner, LANES)
+    around = jnp.concatenate([prof_t[tile], prof_t[tile + 1], prof_t[tile + 2]], axis=1)
+    env[...] = pltpu.roll(around, lax.rem(3 * LANES - lead, 3 * LANES), 1)[:, : 2 * LANES]
     ro = jnp.broadcast_to(ro_col[...], (chans, LANES))
 
     for buf in (x0, x1, gs, gs1):
@@ -414,11 +416,8 @@
         (jnp.zeros((chans, LANES), jnp.float32), jnp.zeros((chans, 2 * LANES), jnp.float32)),
     )
     near = far[:, :LANES] + near
-    zero = jnp.zeros((chans, LANES), jnp.float32)
     whole = jnp.concatenate([near, far[:, LANES:], zero], axis=1)
-    corner = first + LANES
-    tile = corner // LANES
-    whole = pltpu.roll(whole, lax.rem(corner, LANES), 1)
+    whole = pltpu.roll(whole, lead, 1)
     for b in range(gpad.shape[0]):
         gpad[b] = zero
     for b in range(3):
@@ -429,15 +428,14 @@
     for n in range(tcot.shape[0]):
         p, q = pairs[n, 0], pairs[n, 1]
         first_rows = prof[pl.ds(pl.multiple_of(p * LANES + row_start, 8), rows_trans), :] * ro_row[...]
-        second = prof[pl.ds(pl.multiple_of(q * LANES, 8), LANES), :]
         row_pos = p * LANES + row_start + lax.broadcasted_iota(jnp.int32, (rows_trans, LANES), 0)
         col_pos = q * LANES + lax.broadcasted_iota(jnp.int32, (rows_trans, LANES), 1)
         cross = (end_of(row_pos) != end_of(col_pos)).astype(jnp.float32)
-        maps[n] = mm(first_rows, second, NT, EXACT) * cross
+        maps[n] = mm(first_rows, prof_t[1 + q], NN, EXACT) * cross
         spent[...] = jnp.zeros_like(spent)
         spent[pl.ds(row_start, rows_trans), :] = tcot[n] * cross
-        to_first = mm(prof_t[q], spent[...], NT, EXACT) * ro
-        to_second = mm(prof_t[p] * ro, spent[...], NN, EXACT)
+        to_first = mm(prof_t[1 + q], spent[...], NT, EXACT) * ro
+        to_second = mm(prof_t[1 + p] * ro, spent[...], NN, EXACT)
         gpad[1 + p] = gpad[1 + p] + to_first
         gpad[1 + q] = gpad[1 + q] + to_second
 
@@ -448,8 +446,8 @@
     for c in range(chan_count):
         total_proj = jnp.zeros((chans, width), jnp.float32)
         for b in range(seq_count):
-            block = feats[c, (b + 1) * LANES : (b + 2) * LANES, :]
-            total_proj = total_proj + mm(pieces[b][0], block) + mm(pieces[b][1], block)
+            block = feats[c, b]
+            total_proj = total_proj + mm(pieces[b][0], block, NT) + mm(pieces[b][1], block, NT)
         blank = jnp.zeros((chans, LANES - width), jnp.float32)
         misc[c] = (rest[c] + jnp.concatenate([total_proj, blank], axis=1)).astype(jnp.bfloat16)
 
@@ -476,9 +474,9 @@
     gathered = pl.pallas_call(
         gather_kernel,
         out_shape=(
-            shape((chan_count, (seq_count + 3) * bin_dev, width), bf16),
+            shape((chan_count, seq_count, width, bin_dev), bf16),
             shape((chan_count, chans, width), bf16),
-            shape((chan_count, layers, chans, chan_dev), bf16),
+            shape((chan_count, layers, chan_dev, chans), bf16),
             shape((chan_count, layers, chan_dev, 9), f32),
             shape((HALO, bin_dev), f32),
             shape((band_dev, bin_dev), f32),
@@ -490,7 +488,7 @@
             *sems(seq_count * chan_count - 1), *sems(3 * (chan_count - 1)), *sems(3)
         ],
         compiler_params=pltpu.CompilerParams(collective_id=0, has_side_effects=True),
-    )(features, proj_t, mix, kernel, contact_cot)
+    )(features.T, proj_t, mix.transpose(0, 2, 1), kernel, contact_cot)
     feats, projs, mixes, taps, edge, side, side_edge = gathered
 
     field = pltpu.VMEM((2 * LOW + rows, chans, LANES), f32)
@@ -511,7 +509,7 @@
             pltpu.VMEM((2 * layers, wide, wide), bf16),
             pltpu.VMEM((chans, 2 * LANES), f32),
             pltpu.VMEM((total, chans), f32),
-            pltpu.VMEM((seq_count, chans, LANES), f32),
+            pltpu.VMEM((seq_count + 3, chans, LANES), f32),
             field,
             field,
             pltpu.VMEM((layers, rows, chans, LANES), bf16),
@@ -526,6 +524,7 @@
             pltpu.VMEM((band_dev + HALO, LANES), f32),
             pltpu.VMEM((band_dev + HALO, LANES), f32),
             pltpu.VMEM((chan_count, chans, LANES), f32),
+            pltpu.VMEM((chans, chans), f32),
         ],
         compiler_params=pltpu.CompilerParams(vmem_limit_bytes=48 * 1024 * 1024),
     )(
@@ -536,10 +535,10 @@
         reduce_kernel,
         out_shape=(
             shape((band_dev, LANES), f32),
-            shape((bin_dev, width), f32),
-            shape((width, chans), f32),
+            shape((width, bin_dev), f32),
+            shape((chans, width), f32),
             shape((layers, chan_dev, 9), f32),
-            shape((layers, chans, chan_dev), f32),
+            shape((layers, chan_dev, chans), f32),
         ),
         in_specs=[vmem] * 4,
         out_specs=(vmem,) * 5,
@@ -554,7 +553,7 @@
         ],
         compiler_params=pltpu.CompilerParams(collective_id=1, has_side_effects=True),
     )(part, misc, contact, proj_t)
-    return (contact, maps, grad_features, grad_proj, grad_kernel, grad_mix)
+    return (contact, maps, grad_features.T, grad_proj.T, grad_kernel, grad_mix.transpose(0, 2, 1))
 
 
 def solution(mesh):

time: 72.6 us -> 64.9 us (0.89)
  local copies, waits for them, and re-layouts: 16.4 us -> 12.1 us
  Pallas kernels: 54.6 us -> 51.2 us
    unnamed x49 -> x47, local copies, waits for them, and re-layouts: 16.3 us -> 12 us
    pallas_call x1, Pallas kernels: 14 us -> 11.1 us  [per_device(): pl.pallas_call(gather_kernel, out_shape=(shape((chan_count, seq_count, wi...]
where the time goes in v3:
time: 64.9 us; the launch traced here: 64 us
  Pallas kernels  51.2 us (79%)
  local copies, waits for them, and re-layouts  12.1 us (19%)
  between operations  0.74 us (1%)
    pallas_call x1, Pallas kernels, per_device(): pl.pallas_call(band_kernel, out_shape=(shape((band_dev, LANES), f32), sha...  28.8 us
    unnamed x47, local copies, waits for them, and re-layouts  12 us
    pallas_call x1, Pallas kernels, per_device(): pl.pallas_call(reduce_kernel, out_shape=(shape((band_dev, LANES), f32), s...  11.2 us
    pallas_call x1, Pallas kernels, per_device(): pl.pallas_call(gather_kernel, out_shape=(shape((chan_count, seq_count, wi...  11.1 us

profile of v3, /device:TPU:0, one launch (start us, length us, event | category | flops | bytes accessed | tf_op | source)
XLA Modules:
  0.0 64.0 jit_solution(7601196089634739008)
XLA Ops:
  0.6 0.0 copy-start.19
  0.6 0.0 copy-start.12
  0.7 0.8 %copy.17.pairs = s32[4,2]{1,0:T(4,128)S(1)} copy(s32[4,2]{0,1:T(2,128)} %param.17) | data formatting | bytes 64 | tf_op args[7]
  1.4 0.0 copy-done.19
  1.4 0.0 copy-start.2
  1.4 0.7 %copy.16.taps = f32[2,16,9]{2,1,0:T(8,128)} copy(f32[2,16,9]{1,0,2:T(2,128)S(1)} %copy-done.19) | data formatting | bytes 2304 | tf_op args[2]
  2.1 0.0 copy-done.12
  2.1 0.1 copy.18.ro_col
  2.2 11.1 %shard_map.145 = (bf16[2,4,48,128]{3,2,1,0:T(8,128)(2,1)}, bf16[2,32,48]{2,1,0:T(8,128)(2,1)}, bf16[2,2,16,32]{3,2,1,0:T(8,128)(2,1)}, f32[2,2,16,9]{3,2,1,0:T(8...) custom-call(bf16[48,128]{1,0:T(8,128)(2,1)} %bitcast.15, bf16[32,48]{1,0:T(8,128)(2,1)} %bitcast.10, ...), custom_call_target="tpu_custom_call" | custom-call | tf_op jit(solution)/shard_map/pallas_call | solution.py:474
  13.3 0.0 copy-start.11
  13.3 0.0 copy-start.10
  13.4 0.0 copy-start.13
  13.4 0.0 copy-start.14
  13.4 0.0 copy-done.2
  13.4 0.0 copy-done
  13.4 0.6 copy-done.11
  14.0 0.0 copy-done.10
  14.0 0.0 copy-done.13
  14.0 0.0 copy-done.14
  14.0 0.0 copy-start.1
  14.0 0.9 %copy-done.1 = bf16[2,4,48,128]{3,2,1,0:T(8,128)(2,1)S(1)} copy-done((bf16[2,4,48,128]{3,2,1,0:T(8,128)(2,1)S(1)}, bf16[2,4,48,128]{3,2,1,0:T(8,128)(2,1)}, u32[]{:S(2)}) %copy-start.1) | copy-done | bytes 98328
  14.9 0.0 copy-start.3
  14.9 0.8 %copy-done.3 = f32[2,2,16,9]{3,2,1,0:T(8,128)S(1)} copy-done((f32[2,2,16,9]{3,2,1,0:T(8,128)S(1)}, f32[2,2,16,9]{3,2,1,0:T(8,128)}, u32[]{:S(2)}) %copy-start.3) | copy-done | bytes 2328
  15.7 0.0 copy-start.4
  15.7 0.8 %copy-done.4 = f32[64,128]{1,0:T(8,128)S(1)} copy-done((f32[64,128]{1,0:T(8,128)S(1)}, f32[64,128]{1,0:T(8,128)}, u32[]{:S(2)}) %copy-start.4) | copy-done | bytes 32792
  16.4 0.0 copy-start.7
  16.4 0.7 %copy-done.7 = bf16[2,32,48]{2,1,0:T(8,128)(2,1)S(1)} copy-done((bf16[2,32,48]{2,1,0:T(8,128)(2,1)S(1)}, bf16[2,32,48]{2,1,0:T(8,128)(2,1)}, u32[]{:S(2)}) %copy-start.7) | copy-done | bytes 6168
  17.2 0.0 copy-start.8
  17.2 0.7 %copy-done.8 = bf16[2,2,16,32]{3,2,1,0:T(8,128)(2,1)S(1)} copy-done((bf16[2,2,16,32]{3,2,1,0:T(8,128)(2,1)S(1)}, bf16[2,2,16,32]{3,2,1,0:T(8,128)(2,1)}, u32[]{:S(2)}) %copy-start.8) | copy-done | bytes 4120
  17.9 28.8 %shard_map.146 = (f32[64,128]{1,0:T(8,128)S(1)}, f32[4,32,128]{2,1,0:T(8,128)}, bf16[4,32,128]{2,1,0:T(8,128)(2,1)S(1)}, bf16[2,32,128]{2,1,0:T(8,128)(2,1)S(1)}) custom-call(s32[2]{0:T(128)S(1)} %copy-done.13, s32[4]{0:T(128)S(1)} %copy-done.14, s32[4,2]{1,0:T(4,128)S(1)} %copy.17.pairs, bf16[2,4,48,128]{3,2,1,0:T(8,128)(2,1)S(1)} %copy-done.1, ...), custom_call_target="tpu_custom_call" | custom-call | tf_op jit(solution)/shard_map/pallas_call | solution.py:497
  46.7 0.0 copy-start.5
  46.7 0.6 copy-done.5
  47.3 0.0 copy-start.6
  47.3 0.6 copy-done.6
  47.9 0.0 copy-start.9
  47.9 0.6 copy-done.9
  48.5 11.2 %shard_map.147 = (f32[64,128]{1,0:T(8,128)}, f32[48,128]{1,0:T(8,128)}, f32[32,48]{1,0:T(8,128)}, f32[2,16,9]{2,1,0:T(8,128)}, f32[2,16,32]{2,1,0:T(8,128)}) custom-call(bf16[4,32,128]{2,1,0:T(8,128)(2,1)} %copy-done.6, bf16[2,32,128]{2,1,0:T(8,128)(2,1)} %copy-done.9, f32[64,128]{1,0:T(8,128)} %copy-done.5, bf16[32,48]{1,0:T(8,128)(2,1)} %bitcast.11), custom_call_target="tpu_custom_call" | custom-call | tf_op jit(solution)/shard_map/pallas_call | solution.py:534
  59.8 0.0 copy-start.15
  59.8 1.4 %copy.19 = f32[2,16,9]{1,0,2:T(2,128)} copy(f32[2,16,9]{2,1,0:T(8,128)} %get-tuple-element.42) | data formatting | bytes 2304
  61.2 0.0 copy-done.15
  61.2 0.0 copy-start.16
  61.2 0.6 copy.24
  61.8 0.1 copy-done.16
  62.0 0.6 copy.25
  62.6 0.1 copy-done.18
  62.7 0.6 copy.26
  63.3 0.1 copy-done.17
  63.4 0.6 copy.27
  (3 shorter events, 0.0 us)
Async XLA Ops:
  0.6 0.8 %copy-start.19 = (f32[2,16,9]{1,0,2:T(2,128)S(1)}, f32[2,16,9]{1,0,2:T(2,128)}, u32[]{:S(2)}) copy-start(f32[2,16,9]{1,0,2:T(2,128)} %param.12) | copy-start | bytes 3460
  0.6 1.5 %copy-start.12 = (f32[32]{0:T(128)S(1)}, f32[32]{0:T(128)}, u32[]{:S(2)}) copy-start(f32[32]{0:T(128)} %param.14) | copy-start | bytes 388
  1.4 12.0 %copy-start.2 = (f32[4,32,128]{2,1,0:T(8,128)S(1)}, f32[4,32,128]{2,1,0:T(8,128)}, u32[]{:S(2)}) copy-start(f32[4,32,128]{2,1,0:T(8,128)} %tcot.1) | copy-start | bytes 196612
  2.2 11.2 %copy-start = (f32[64,128]{1,0:T(8,128)S(1)}, f32[64,128]{1,0:T(8,128)}, u32[]{:S(2)}) copy-start(f32[64,128]{1,0:T(8,128)} %cot_own.1) | copy-start | bytes 98308
  13.3 0.7 %copy-start.11 = (f32[8,128]{1,0:T(8,128)S(1)}, f32[8,128]{1,0:T(8,128)}, u32[]{:S(2)}) copy-start(f32[8,128]{1,0:T(8,128)} %get-tuple-element.28.cot_side_edge) | copy-start | bytes 12292
  13.3 0.7 %copy-start.10 = (f32[8,128]{1,0:T(8,128)S(1)}, f32[8,128]{1,0:T(8,128)}, u32[]{:S(2)}) copy-start(f32[8,128]{1,0:T(8,128)} %get-tuple-element.26.cot_edge) | copy-start | bytes 12292
  13.4 0.7 %copy-start.13 = (s32[2]{0:T(128)S(1)}, s32[2]{0:T(128)}, u32[]{:S(2)}) copy-start(s32[2]{0:T(128)} %dil.1) | copy-start | bytes 28
  13.4 0.7 %copy-start.14 = (s32[4]{0:T(128)S(1)}, s32[4]{0:T(128)}, u32[]{:S(2)}) copy-start(s32[4]{0:T(128)} %chroms.1) | copy-start | bytes 52
  14.0 0.9 %copy-start.1 = (bf16[2,4,48,128]{3,2,1,0:T(8,128)(2,1)S(1)}, bf16[2,4,48,128]{3,2,1,0:T(8,128)(2,1)}, u32[]{:S(2)}) copy-start(bf16[2,4,48,128]{3,2,1,0:T(8,128)(2,1)} %get-tuple-element.22.feats) | copy-start | bytes 294916
  14.9 0.8 %copy-start.3 = (f32[2,2,16,9]{3,2,1,0:T(8,128)S(1)}, f32[2,2,16,9]{3,2,1,0:T(8,128)}, u32[]{:S(2)}) copy-start(f32[2,2,16,9]{3,2,1,0:T(8,128)} %get-tuple-element.25.taps_in) | copy-start | bytes 6916
  15.7 0.8 %copy-start.4 = (f32[64,128]{1,0:T(8,128)S(1)}, f32[64,128]{1,0:T(8,128)}, u32[]{:S(2)}) copy-start(f32[64,128]{1,0:T(8,128)} %get-tuple-element.27.cot_side) | copy-start | bytes 98308
  16.4 0.7 %copy-start.7 = (bf16[2,32,48]{2,1,0:T(8,128)(2,1)S(1)}, bf16[2,32,48]{2,1,0:T(8,128)(2,1)}, u32[]{:S(2)}) copy-start(bf16[2,32,48]{2,1,0:T(8,128)(2,1)} %get-tuple-element.23.projs) | copy-start | bytes 18436
  17.2 0.7 %copy-start.8 = (bf16[2,2,16,32]{3,2,1,0:T(8,128)(2,1)S(1)}, bf16[2,2,16,32]{3,2,1,0:T(8,128)(2,1)}, u32[]{:S(2)}) copy-start(bf16[2,2,16,32]{3,2,1,0:T(8,128)(2,1)} %get-tuple-element.24.mixes) | copy-start | bytes 12292
  46.7 0.6 copy-start.5
  47.3 0.6 copy-start.6
  47.9 0.6 copy-start.9
  59.8 1.4 %copy-start.15 = (f32[64,128]{1,0:T(8,128)S(1)}, f32[64,128]{1,0:T(8,128)}, u32[]{:S(2)}) copy-start(f32[64,128]{1,0:T(8,128)} %get-tuple-element.50) | copy-start | bytes 98308
  61.2 0.8 %copy-start.16 = (f32[48,128]{1,0:T(8,128)S(1)}, f32[48,128]{1,0:T(8,128)}, u32[]{:S(2)}) copy-start(f32[48,128]{1,0:T(8,128)} %get-tuple-element.34) | copy-start | bytes 73732
  62.0 0.7 %copy-start.18 = (f32[32,48]{1,0:T(8,128)S(1)}, f32[32,48]{1,0:T(8,128)}, u32[]{:S(2)}) copy-start(f32[32,48]{1,0:T(8,128)} %get-tuple-element.35) | copy-start | bytes 18436
  62.7 0.7 %copy-start.17 = (f32[2,16,32]{2,1,0:T(8,128)S(1)}, f32[2,16,32]{2,1,0:T(8,128)}, u32[]{:S(2)}) copy-start(f32[2,16,32]{2,1,0:T(8,128)} %get-tuple-element.37) | copy-start | bytes 12292

commit v4 on v3

--- a/solution.py
+++ b/solution.py
@@ -278,7 +278,7 @@
         x0[LOW + i] = env[:, :LANES] * moved * mask(i)
         return 0
 
-    lax.fori_loop(0, rows, build, 0, unroll=4)
+    lax.fori_loop(0, rows, build, 0, unroll=8)
 
     def conv(x, l, d, r, sign):
         lines = [x[LOW + r + sign * b * d] for b in (-1, 0, 1)]
@@ -299,10 +299,12 @@
 
         def layer(i, _, l=l, d=d, x=x, base=base):
             r0 = base + i * BATCH
+            hidden = []
             for j in range(BATCH):
                 summed = conv(x, l, d, r0 + j, 1)
-                h[l, r0 + j] = jnp.maximum(summed, 0.0).astype(jnp.bfloat16)
-            upd = mm(spread[2 * l], h[l, pl.ds(r0, BATCH)].reshape(wide, LANES))
+                hidden.append(jnp.maximum(summed, 0.0).astype(jnp.bfloat16))
+                h[l, r0 + j] = hidden[j]
+            upd = mm(spread[2 * l], jnp.concatenate(hidden, axis=0))
             upd = upd.reshape(BATCH, chans, LANES)
             for j in range(BATCH):
                 new = (x[LOW + r0 + j] + upd[j]) * mask(r0 + j)
@@ -312,7 +314,7 @@
                     picture[pl.ds(i * BATCH + j, 1), :] = jnp.sum(new * ro, axis=0, keepdims=True)
             return 0
 
-        lax.fori_loop(0, (rows - HALO * (l + 1)) // BATCH, layer, 0)
+        lax.fori_loop(0, (rows - HALO * (l + 1)) // BATCH, layer, 0, unroll=2)
 
     shown = picture[pl.ds(own_at, own_rows), :] * own_lane
     contact[...] = pltpu.roll(shown, lax.rem(LANES - turn, LANES), 1)
@@ -320,8 +322,7 @@
         rest[c] = jnp.zeros((chans, LANES), jnp.float32)
 
     def pull(l, r0, source, target):
-        g = source[pl.ds(r0, BATCH)].reshape(wide, LANES)
-        high, low = split(g)
+        high, low = split(jnp.concatenate(source, axis=0))
         gh = mm(spread[2 * l + 1], high) + mm(spread[2 * l + 1], low)
         gh = gh.astype(jnp.bfloat16).astype(jnp.float32).reshape(BATCH, chans, LANES)
         for j in range(BATCH):
@@ -359,13 +360,15 @@
 
     def last_out(i, _):
         r0 = sub_pos * 2 * HALO + i * BATCH
+        lines = []
         for j in range(BATCH):
             line = cot[pl.ds(i * BATCH + j, 1), :] * mask(r0 + j)
-            go[r0 + j] = ro * line
-        pull(1, r0, go, gs)
+            lines.append(ro * line)
+            go[r0 + j] = lines[j]
+        pull(1, r0, lines, gs)
         return 0
 
-    lax.fori_loop(0, (rows - 2 * HALO) // BATCH, last_out, 0)
+    lax.fori_loop(0, (rows - 2 * HALO) // BATCH, last_out, 0, unroll=3)
     weight_grads(1, x1, dil[1], go, gs)
 
     def fold(l, d, g, target):
@@ -383,12 +386,14 @@
 
     def first_out(i, _):
         r0 = own_start + i * BATCH
+        lines = []
         for j in range(BATCH):
-            go1[r0 + j] = gf[r0 + j] * (mask(r0 + j) * own_lane)
-        pull(0, r0, go1, gs1)
+            lines.append(gf[r0 + j] * (mask(r0 + j) * own_lane))
+            go1[r0 + j] = lines[j]
+        pull(0, r0, lines, gs1)
         return 0
 
-    lax.fori_loop(0, own_rows // BATCH, first_out, 0)
+    lax.fori_loop(0, own_rows // BATCH, first_out, 0, unroll=2)
     weight_grads(0, x0, dil[0], go1, gs1)
 
     def back_first(i, _):
@@ -414,6 +419,7 @@
     near, far = lax.fori_loop(
         0, rows - 2 * HALO, to_profile,
         (jnp.zeros((chans, LANES), jnp.float32), jnp.zeros((chans, 2 * LANES), jnp.float32)),
+        unroll=8,
     )
     near = far[:, :LANES] + near
     whole = jnp.concatenate([near, far[:, LANES:], zero], axis=1)

time: 64.9 us -> 56 us (0.86)
  Pallas kernels: 51.2 us -> 42.4 us
    pallas_call x1, Pallas kernels: 28.8 us -> 20 us  [per_device(): pl.pallas_call(band_kernel, out_shape=(shape((band_dev, LANES), f32), sha...]
where the time goes in v4:
time: 56 us; the launch traced here: 55.2 us
  Pallas kernels  42.4 us (76%)
  local copies, waits for them, and re-layouts  12.1 us (22%)
  between operations  0.74 us (1%)
    pallas_call x1, Pallas kernels, per_device(): pl.pallas_call(band_kernel, out_shape=(shape((band_dev, LANES), f32), sha...  20 us
    unnamed x47, local copies, waits for them, and re-layouts  12 us
    pallas_call x1, Pallas kernels, per_device(): pl.pallas_call(reduce_kernel, out_shape=(shape((band_dev, LANES), f32), s...  11.2 us
    pallas_call x1, Pallas kernels, per_device(): pl.pallas_call(gather_kernel, out_shape=(shape((chan_count, seq_count, wi...  11.1 us

profile of v4, /device:TPU:0, one launch (start us, length us, event | category | flops | bytes accessed | tf_op | source)
XLA Modules:
  0.0 55.2 jit_solution(9651452313872142180)
XLA Ops:
  0.6 0.0 copy-start.19
  0.6 0.0 copy-start.12
  0.7 0.8 %copy.17.pairs = s32[4,2]{1,0:T(4,128)S(1)} copy(s32[4,2]{0,1:T(2,128)} %param.17) | data formatting | bytes 64 | tf_op args[7]
  1.4 0.0 copy-done.19
  1.4 0.0 copy-start.2
  1.4 0.7 %copy.16.taps = f32[2,16,9]{2,1,0:T(8,128)} copy(f32[2,16,9]{1,0,2:T(2,128)S(1)} %copy-done.19) | data formatting | bytes 2304 | tf_op args[2]
  2.1 0.0 copy-done.12
  2.1 0.1 copy.18.ro_col
  2.2 0.0 copy-start
  2.2 11.1 %shard_map.145 = (bf16[2,4,48,128]{3,2,1,0:T(8,128)(2,1)}, bf16[2,32,48]{2,1,0:T(8,128)(2,1)}, bf16[2,2,16,32]{3,2,1,0:T(8,128)(2,1)}, f32[2,2,16,9]{3,2,1,0:T(8...) custom-call(bf16[48,128]{1,0:T(8,128)(2,1)} %bitcast.15, bf16[32,48]{1,0:T(8,128)(2,1)} %bitcast.10, ...), custom_call_target="tpu_custom_call" | custom-call | tf_op jit(solution)/shard_map/pallas_call | solution.py:480
  13.3 0.0 copy-start.11
  13.3 0.0 copy-start.10
  13.4 0.0 copy-start.13
  13.4 0.0 copy-start.14
  13.4 0.0 copy-done.2
  13.4 0.0 copy-done
  13.4 0.6 %copy-done.11 = f32[8,128]{1,0:T(8,128)S(1)} copy-done((f32[8,128]{1,0:T(8,128)S(1)}, f32[8,128]{1,0:T(8,128)}, u32[]{:S(2)}) %copy-start.11) | copy-done | bytes 4120
  14.0 0.0 copy-done.10
  14.0 0.0 copy-done.13
  14.0 0.0 copy-done.14
  14.0 0.0 copy-start.1
  14.0 0.9 %copy-done.1 = bf16[2,4,48,128]{3,2,1,0:T(8,128)(2,1)S(1)} copy-done((bf16[2,4,48,128]{3,2,1,0:T(8,128)(2,1)S(1)}, bf16[2,4,48,128]{3,2,1,0:T(8,128)(2,1)}, u32[]{:S(2)}) %copy-start.1) | copy-done | bytes 98328
  14.9 0.0 copy-start.3
  14.9 0.8 %copy-done.3 = f32[2,2,16,9]{3,2,1,0:T(8,128)S(1)} copy-done((f32[2,2,16,9]{3,2,1,0:T(8,128)S(1)}, f32[2,2,16,9]{3,2,1,0:T(8,128)}, u32[]{:S(2)}) %copy-start.3) | copy-done | bytes 2328
  15.7 0.0 copy-start.4
  15.7 0.8 %copy-done.4 = f32[64,128]{1,0:T(8,128)S(1)} copy-done((f32[64,128]{1,0:T(8,128)S(1)}, f32[64,128]{1,0:T(8,128)}, u32[]{:S(2)}) %copy-start.4) | copy-done | bytes 32792
  16.4 0.0 copy-start.7
  16.4 0.7 %copy-done.7 = bf16[2,32,48]{2,1,0:T(8,128)(2,1)S(1)} copy-done((bf16[2,32,48]{2,1,0:T(8,128)(2,1)S(1)}, bf16[2,32,48]{2,1,0:T(8,128)(2,1)}, u32[]{:S(2)}) %copy-start.7) | copy-done | bytes 6168
  17.2 0.0 copy-start.8
  17.2 0.7 %copy-done.8 = bf16[2,2,16,32]{3,2,1,0:T(8,128)(2,1)S(1)} copy-done((bf16[2,2,16,32]{3,2,1,0:T(8,128)(2,1)S(1)}, bf16[2,2,16,32]{3,2,1,0:T(8,128)(2,1)}, u32[]{:S(2)}) %copy-start.8) | copy-done | bytes 4120
  17.9 20.0 %shard_map.146 = (f32[64,128]{1,0:T(8,128)S(1)}, f32[4,32,128]{2,1,0:T(8,128)}, bf16[4,32,128]{2,1,0:T(8,128)(2,1)S(1)}, bf16[2,32,128]{2,1,0:T(8,128)(2,1)S(1)}) custom-call(s32[2]{0:T(128)S(1)} %copy-done.13, s32[4]{0:T(128)S(1)} %copy-done.14, s32[4,2]{1,0:T(4,128)S(1)} %copy.17.pairs, bf16[2,4,48,128]{3,2,1,0:T(8,128)(2,1)S(1)} %copy-done.1, ...), custom_call_target="tpu_custom_call" | custom-call | tf_op jit(solution)/shard_map/pallas_call | solution.py:503
  37.9 0.0 copy-start.5
  37.9 0.6 %copy-done.5 = f32[64,128]{1,0:T(8,128)} copy-done((f32[64,128]{1,0:T(8,128)}, f32[64,128]{1,0:T(8,128)S(1)}, u32[]{:S(2)}) %copy-start.5) | copy-done | bytes 32792
  38.5 0.0 copy-start.6
  38.5 0.6 %copy-done.6 = bf16[4,32,128]{2,1,0:T(8,128)(2,1)} copy-done((bf16[4,32,128]{2,1,0:T(8,128)(2,1)}, bf16[4,32,128]{2,1,0:T(8,128)(2,1)S(1)}, u32[]{:S(2)}) %copy-start.6) | copy-done | bytes 32792
  39.1 0.0 copy-start.9
  39.1 0.6 %copy-done.9 = bf16[2,32,128]{2,1,0:T(8,128)(2,1)} copy-done((bf16[2,32,128]{2,1,0:T(8,128)(2,1)}, bf16[2,32,128]{2,1,0:T(8,128)(2,1)S(1)}, u32[]{:S(2)}) %copy-start.9) | copy-done | bytes 16408
  39.7 11.2 %shard_map.147 = (f32[64,128]{1,0:T(8,128)}, f32[48,128]{1,0:T(8,128)}, f32[32,48]{1,0:T(8,128)}, f32[2,16,9]{2,1,0:T(8,128)}, f32[2,16,32]{2,1,0:T(8,128)}) custom-call(bf16[4,32,128]{2,1,0:T(8,128)(2,1)} %copy-done.6, bf16[2,32,128]{2,1,0:T(8,128)(2,1)} %copy-done.9, f32[64,128]{1,0:T(8,128)} %copy-done.5, bf16[32,48]{1,0:T(8,128)(2,1)} %bitcast.11), custom_call_target="tpu_custom_call" | custom-call | tf_op jit(solution)/shard_map/pallas_call | solution.py:540
  51.0 0.0 copy-start.15
  51.0 1.4 %copy.19 = f32[2,16,9]{1,0,2:T(2,128)} copy(f32[2,16,9]{2,1,0:T(8,128)} %get-tuple-element.42) | data formatting | bytes 2304
  52.4 0.0 copy-done.15
  52.4 0.6 %copy.24 = f32[64,128]{1,0:T(8,128)} copy(f32[64,128]{1,0:T(8,128)S(1)} %copy-done.15) | data formatting | bytes 65536
  53.0 0.1 copy-done.16
  53.1 0.6 %copy.25 = f32[128,48]{0,1:T(8,128)} copy(f32[128,48]{0,1:T(8,128)S(1)} %bitcast.12) | data formatting | bytes 49152
  53.8 0.1 copy-done.18
  53.9 0.6 %copy.26 = f32[48,32]{0,1:T(8,128)} copy(f32[48,32]{0,1:T(8,128)S(1)} %bitcast.14) | data formatting | bytes 12288
  54.5 0.1 copy-done.17
  54.6 0.6 %copy.27 = f32[2,32,16]{1,2,0:T(8,128)} copy(f32[2,32,16]{1,2,0:T(8,128)S(1)} %bitcast.13) | data formatting | bytes 8192
  (3 shorter events, 0.0 us)
Async XLA Ops:
  0.6 0.8 %copy-start.19 = (f32[2,16,9]{1,0,2:T(2,128)S(1)}, f32[2,16,9]{1,0,2:T(2,128)}, u32[]{:S(2)}) copy-start(f32[2,16,9]{1,0,2:T(2,128)} %param.12) | copy-start | bytes 3460
  0.6 1.5 %copy-start.12 = (f32[32]{0:T(128)S(1)}, f32[32]{0:T(128)}, u32[]{:S(2)}) copy-start(f32[32]{0:T(128)} %param.14) | copy-start | bytes 388
  1.4 12.0 %copy-start.2 = (f32[4,32,128]{2,1,0:T(8,128)S(1)}, f32[4,32,128]{2,1,0:T(8,128)}, u32[]{:S(2)}) copy-start(f32[4,32,128]{2,1,0:T(8,128)} %tcot.1) | copy-start | bytes 196612
  2.2 11.2 %copy-start = (f32[64,128]{1,0:T(8,128)S(1)}, f32[64,128]{1,0:T(8,128)}, u32[]{:S(2)}) copy-start(f32[64,128]{1,0:T(8,128)} %cot_own.1) | copy-start | bytes 98308
  13.3 0.7 %copy-start.11 = (f32[8,128]{1,0:T(8,128)S(1)}, f32[8,128]{1,0:T(8,128)}, u32[]{:S(2)}) copy-start(f32[8,128]{1,0:T(8,128)} %get-tuple-element.28.cot_side_edge) | copy-start | bytes 12292
  13.3 0.7 %copy-start.10 = (f32[8,128]{1,0:T(8,128)S(1)}, f32[8,128]{1,0:T(8,128)}, u32[]{:S(2)}) copy-start(f32[8,128]{1,0:T(8,128)} %get-tuple-element.26.cot_edge) | copy-start | bytes 12292
  13.4 0.7 %copy-start.13 = (s32[2]{0:T(128)S(1)}, s32[2]{0:T(128)}, u32[]{:S(2)}) copy-start(s32[2]{0:T(128)} %dil.1) | copy-start | bytes 28
  13.4 0.7 %copy-start.14 = (s32[4]{0:T(128)S(1)}, s32[4]{0:T(128)}, u32[]{:S(2)}) copy-start(s32[4]{0:T(128)} %chroms.1) | copy-start | bytes 52
  14.0 0.9 %copy-start.1 = (bf16[2,4,48,128]{3,2,1,0:T(8,128)(2,1)S(1)}, bf16[2,4,48,128]{3,2,1,0:T(8,128)(2,1)}, u32[]{:S(2)}) copy-start(bf16[2,4,48,128]{3,2,1,0:T(8,128)(2,1)} %get-tuple-element.22.feats) | copy-start | bytes 294916
  14.9 0.8 %copy-start.3 = (f32[2,2,16,9]{3,2,1,0:T(8,128)S(1)}, f32[2,2,16,9]{3,2,1,0:T(8,128)}, u32[]{:S(2)}) copy-start(f32[2,2,16,9]{3,2,1,0:T(8,128)} %get-tuple-element.25.taps_in) | copy-start | bytes 6916
  15.7 0.8 %copy-start.4 = (f32[64,128]{1,0:T(8,128)S(1)}, f32[64,128]{1,0:T(8,128)}, u32[]{:S(2)}) copy-start(f32[64,128]{1,0:T(8,128)} %get-tuple-element.27.cot_side) | copy-start | bytes 98308
  16.4 0.7 %copy-start.7 = (bf16[2,32,48]{2,1,0:T(8,128)(2,1)S(1)}, bf16[2,32,48]{2,1,0:T(8,128)(2,1)}, u32[]{:S(2)}) copy-start(bf16[2,32,48]{2,1,0:T(8,128)(2,1)} %get-tuple-element.23.projs) | copy-start | bytes 18436
  17.2 0.7 %copy-start.8 = (bf16[2,2,16,32]{3,2,1,0:T(8,128)(2,1)S(1)}, bf16[2,2,16,32]{3,2,1,0:T(8,128)(2,1)}, u32[]{:S(2)}) copy-start(bf16[2,2,16,32]{3,2,1,0:T(8,128)(2,1)} %get-tuple-element.24.mixes) | copy-start | bytes 12292
  37.9 0.6 %copy-start.5 = (f32[64,128]{1,0:T(8,128)}, f32[64,128]{1,0:T(8,128)S(1)}, u32[]{:S(2)}) copy-start(f32[64,128]{1,0:T(8,128)S(1)} %get-tuple-element.31.contact) | copy-start | bytes 98308
  38.5 0.6 %copy-start.6 = (bf16[4,32,128]{2,1,0:T(8,128)(2,1)}, bf16[4,32,128]{2,1,0:T(8,128)(2,1)S(1)}, u32[]{:S(2)}) copy-start(bf16[4,32,128]{2,1,0:T(8,128)(2,1)S(1)} %get-tuple-element.29.part) | copy-start | bytes 98308
  39.1 0.6 %copy-start.9 = (bf16[2,32,128]{2,1,0:T(8,128)(2,1)}, bf16[2,32,128]{2,1,0:T(8,128)(2,1)S(1)}, u32[]{:S(2)}) copy-start(bf16[2,32,128]{2,1,0:T(8,128)(2,1)S(1)} %get-tuple-element.30.misc) | copy-start | bytes 49156
  51.0 1.4 %copy-start.15 = (f32[64,128]{1,0:T(8,128)S(1)}, f32[64,128]{1,0:T(8,128)}, u32[]{:S(2)}) copy-start(f32[64,128]{1,0:T(8,128)} %get-tuple-element.50) | copy-start | bytes 98308
  52.4 0.8 %copy-start.16 = (f32[48,128]{1,0:T(8,128)S(1)}, f32[48,128]{1,0:T(8,128)}, u32[]{:S(2)}) copy-start(f32[48,128]{1,0:T(8,128)} %get-tuple-element.34) | copy-start | bytes 73732
  53.1 0.7 %copy-start.18 = (f32[32,48]{1,0:T(8,128)S(1)}, f32[32,48]{1,0:T(8,128)}, u32[]{:S(2)}) copy-start(f32[32,48]{1,0:T(8,128)} %get-tuple-element.35) | copy-start | bytes 18436
  53.9 0.7 %copy-start.17 = (f32[2,16,32]{2,1,0:T(8,128)S(1)}, f32[2,16,32]{2,1,0:T(8,128)}, u32[]{:S(2)}) copy-start(f32[2,16,32]{2,1,0:T(8,128)} %get-tuple-element.37) | copy-start | bytes 12292
